TPU v7x, 256 devices: a whole 4x4x8 slice. The times are simulated.
256 devices in a mesh: bulk: 16 (over y, z_hi, core), occ: 16 (over x, z_lo).
Axes of the slice: x: 4, y: 4, z: 8 (z_hi: 2, z_lo: 4; z = z_hi * 4 + z_lo), core: 2. Of those that a mesh axis runs over, the one named last changes fastest.
Arguments:
- lambda_cd: bfloat16 [512, 256, 900], P('bulk', 'occ'), may hold values from -6 to 6
- integrals: bfloat16 [256, 900, 4096], P('occ', None, 'bulk'), may hold values from -0.01171875 to 0.01171875
- other_terms: bfloat16 [512, 4096], P('occ', 'bulk'), may hold values from -6 to 6
- hole_energy: float32 [60], replicated, may hold values from 0.3 to 3
- virtual_energy: float32 [64], replicated, may hold values from 0.1 to 3
- pair_orbitals: int32 [512, 2], P('occ'), may hold values from 0 to 59
Outputs:
- new_lambda: float32 [512, 4096], P('occ', 'bulk')
All inputs are finite; a program needn't handle non-finite values.
Results may differ from a plain program's by a relative error of at most 0.0003.
Values may be sent and summed in bfloat16 or wider, within the bound.
No kernel may reach another device: no remote copies, remote signals or barrier semaphores. Data moves between devices by JAX's collectives and lax.ppermute only.
A program may use at most 128 MiB of HBM per device.

v0:
```python
import jax
import jax.numpy as jnp
from jax import lax
from jax.sharding import PartitionSpec as P

VW = 64


def local(lambda_cd, integrals, other_terms, hole_energy, virtual_energy, pair_orbitals):
    c_count, d_count, columns = integrals.shape
    bulk_count = lax.axis_size("bulk")
    own_width = VW // bulk_count
    flat_ints = integrals.reshape(c_count * d_count, columns)
    piece = lax.all_gather(lambda_cd, "bulk", axis=0, tiled=True)
    row_count = piece.shape[0]
    flat_piece = piece.reshape(row_count, c_count * d_count)
    partial_value = jnp.dot(flat_piece, flat_ints, preferred_element_type=jnp.float32)
    summed = lax.psum_scatter(partial_value, "occ", scatter_dimension=0, tiled=True)
    row_count = summed.shape[0]
    blocks = summed.reshape(row_count, own_width, bulk_count, own_width)
    swapped = lax.all_to_all(blocks, "bulk", split_axis=2, concat_axis=1, tiled=True)
    swapped = jnp.transpose(swapped.reshape(row_count, VW, own_width), (0, 2, 1)).reshape(
        row_count, columns
    )
    antisym = summed - swapped
    orbital_ids = jnp.arange(hole_energy.shape[0], dtype=jnp.int32)
    onehot = (pair_orbitals[:, :, None] == orbital_ids[None, None, :]).astype(jnp.float32)
    pair_hole = jnp.sum(onehot * hole_energy[None, None, :], axis=(1, 2))
    a_start = lax.axis_index("bulk") * own_width
    own_virtual = lax.dynamic_slice_in_dim(virtual_energy, a_start, own_width)
    denom = pair_hole[:, None, None] + own_virtual[None, :, None] + virtual_energy[None, None, :]
    denom = denom.reshape(row_count, columns)
    return -(other_terms.astype(jnp.float32) + 0.5 * antisym) / denom


def solution(mesh):
    placed = (
        P("bulk", "occ", None),
        P("occ", None, "bulk"),
        P("occ", "bulk"),
        P(),
        P(),
        P("occ", None),
    )
    return jax.shard_map(
        local, mesh=mesh, in_specs=placed, out_specs=P("occ", "bulk"), check_vma=False
    )
```

profile of v0, /device:TPU:1, one launch (start us, length us, event | category | flops | bytes accessed | tf_op | source)
XLA Modules:
  0.0 312.2 jit_solution(10270793774650243878)
XLA Ops:
  6.5 0.0 all-gather.2.cloned.1.call-start
  6.5 2.8 copy.24
  9.3 0.0 all-gather.2.cloned.1.call-update
  9.3 0.0 copy-start.2
  9.3 0.0 copy-start.1
  9.4 0.0 copy-start.3
  9.4 0.0 copy-start
  9.4 0.0 reduce-scatter.2.cloned.1.call-start
  9.4 179.7 %all-gather.2.cloned.1.call-done = bf16[512,16,900]{2,0,1:T(8,128)(2,1)} async-done(((bf16[32,16,900]{2,0,1:T(8,128)(2,1)}), bf16[512,16,900]{2,0,1:T(8,128)(2,1)}) %all-gather.2.cloned.1.call-update) | async-done | bytes 14745616 | tf_op jit(solution)/shard_map/all_gather | solution.py:14
  189.1 15.5 %fusion.2 = f32[512,256]{1,0:T(8,128)} fusion(bf16[512,16,900]{2,0,1:T(8,128)(2,1)} %all-gather.2.cloned.1.call-done, bf16[16,900,256]{2,0,1:T(8,128)(2,1)} %param.7), kind=kOutput, calls=%fused_computation.2 | convolution fusion | flops 3774873600 | bytes 22642688 | tf_op jit(solution)/shard_map/dot_general | solution.py:17
  204.6 0.0 reduce-scatter.2.cloned.1.call-update
  204.6 0.0 copy-done.2
  204.6 0.1 dynamic_slice.3
  204.7 0.0 copy-done.1
  204.7 0.0 copy-done.3
  204.7 0.2 select_reduce_fusion
  204.9 67.2 %reduce-scatter.2.cloned.1.call-done = f32[32,256]{1,0:T(8,128)} async-done(((f32[512,256]{1,0:T(8,128)}), f32[32,256]{1,0:T(8,128)}) %reduce-scatter.2.cloned.1.call-update) | async-done | bytes 32784 | tf_op jit(solution)/shard_map/reduce_scatter | solution.py:18
  272.1 0.9 copy.26
  273.0 0.8 reshape.54
  273.7 19.0 %all-to-all-start = ((f32[16,1,512]{2,1,0:T(1,128)}), f32[16,1,512]{2,1,0:T(1,128)S(1)}, u32[]{:S(2)}, u32[]{:S(2)}) async-start(f32[16,1,512]{2,1,0:T(1,128)} %reshape.54), calls=%async_computation.1 | async-start | bytes 65536 | tf_op jit(solution)/shard_map/all_to_all | solution.py:21
  292.7 0.1 broadcast_add_fusion
  292.8 0.1 add.51
  292.9 0.1 add.52
  293.0 0.1 add.54
  293.1 9.3 %all-to-all-done = f32[16,1,512]{2,1,0:T(1,128)S(1)} async-done(((f32[16,1,512]{2,1,0:T(1,128)}), f32[16,1,512]{2,1,0:T(1,128)S(1)}, u32[]{:S(2)}, u32[]{:S(2)}) %all-to-all-start) | async-done | bytes 32800 | tf_op jit(solution)/shard_map/all_to_all | solution.py:21
  302.4 0.5 broadcast.34
  303.0 0.7 reduce
  303.7 0.1 reshape.55
  303.9 0.1 copy.30
  303.9 0.0 copy-done
  303.9 1.4 add_divide_fusion
  (4 shorter events, 0.1 us)
Async XLA Ops:
  6.5 182.6 %all-gather.2.cloned.1.call-start = ((), (), s32[]{:S(2)}) async-start(), calls=%async_computation.2 | async-start | bytes 17825792 | tf_op jit(solution)/shard_map/all_gather | solution.py:14
  9.3 195.3 %copy-start.2 = (f32[64]{0:T(128)S(1)}, f32[64]{0:T(128)}, u32[]{:S(2)}) copy-start(f32[64]{0:T(128)} %param.10) | copy-start | bytes 772
  9.3 195.4 %copy-start.1 = (s32[32,2]{0,1:T(2,128)S(1)}, s32[32,2]{0,1:T(2,128)}, u32[]{:S(2)}) copy-start(s32[32,2]{0,1:T(2,128)} %param.11) | copy-start | bytes 772
  9.4 195.4 %copy-start.3 = (f32[60]{0:T(128)S(1)}, f32[60]{0:T(128)}, u32[]{:S(2)}) copy-start(f32[60]{0:T(128)} %param.9) | copy-start | bytes 724
  9.4 294.6 %copy-start = (bf16[32,256]{1,0:T(8,128)(2,1)S(1)}, bf16[32,256]{1,0:T(8,128)(2,1)}, u32[]{:S(2)}) copy-start(bf16[32,256]{1,0:T(8,128)(2,1)} %param.8) | copy-start | bytes 49156
  9.4 262.7 %reduce-scatter.2.cloned.1.call-start = ((), (), s32[]{:S(2)}) async-start(), calls=%async_computation.3 | async-start | bytes 557056 | tf_op jit(solution)/shard_map/reduce_scatter | solution.py:18
  273.7 28.7 %all-to-all-start = ((f32[16,1,512]{2,1,0:T(1,128)}), f32[16,1,512]{2,1,0:T(1,128)S(1)}, u32[]{:S(2)}, u32[]{:S(2)}) async-start(f32[16,1,512]{2,1,0:T(1,128)} %reshape.54), calls=%async_computation.1 | async-start | bytes 65536 | tf_op jit(solution)/shard_map/all_to_all | solution.py:21
Sparse Core Ops, SparseCore 0:
  10.1 178.9 all-gather.1
  204.7 67.3 reduce-scatter.1
where the time goes:
time: 312 us
  waiting for transfers between devices  256 us (82%)
  starting transfers between devices  19 us (6%)
  matrix products  15.5 us (5%)
  between operations  13.5 us (4%)
  local copies, waits for them, and re-layouts  5.53 us (2%)
    all_gather x1, waiting for transfers between devices, local(): piece = lax.all_gather(lambda_cd, 'bulk', axis=0, tiled=True)  180 us
    reduce_scatter x1, waiting for transfers between devices, local(): lax.psum_scatter(partial_value, 'occ', scatter_dimension=0, tiled=True)  67.2 us
    all_to_all x1, starting transfers between devices, local(): lax.all_to_all(blocks, 'bulk', split_axis=2, concat_axis=1, tiled=True)  19 us
    dot_general x1, matrix products, local(): jnp.dot(flat_piece, flat_ints, preferred_element_type=jnp.float32)  15.5 us
    all_to_all x1, waiting for transfers between devices, local(): lax.all_to_all(blocks, 'bulk', split_axis=2, concat_axis=1, tiled=True)  9.35 us
  transfers between devices with their start and end apart: 3, of which 3 were waited for; matrix products, arithmetic and copies ran while one was open for 0% of the time, Pallas kernels for 0%

commit v1 on v0

v1 whole, which is shorter than its diff:
```python
import functools

import jax
import jax.numpy as jnp
from jax import lax
from jax.experimental import pallas as pl
from jax.experimental.pallas import tpu as pltpu
from jax.sharding import PartitionSpec as P

VW = 64
COLS = 256
ROWS = 32
C_HALF = 8
D = 900
K_ALL = C_HALF * D
MIB = 1024 * 1024
COSTS = (10, 10, 10, 10, 10, 10, 10, 10)


def p_of(y, h, core):
    return ((y % 4) * 2 + h % 2) * 2 + core % 2


def bulk_shift(name, value, dy=0, dh=0, dc=0):
    pairs = []
    for y in range(4):
        for h in range(2):
            for core in range(2):
                pairs.append((p_of(y, h, core), p_of(y + dy, h + dh, core + dc)))
    with jax.named_scope(name):
        return lax.ppermute(value, "bulk", pairs)


def after(value, *others):
    return lax.optimization_barrier((value,) + others)[0]


def pack_kernel(core_ref, lam_ref, own_ref, other_ref):
    core = core_ref[0]
    n = ROWS * 16
    row = lax.broadcasted_iota(jnp.int32, (n, n), 0)
    col = lax.broadcasted_iota(jnp.int32, (n, n), 1)
    c = ((row // 256 + core) % 2) * C_HALF + (row % 256) // ROWS
    perm = jnp.where(col == (row % ROWS) * 16 + c, 1.0, 0.0).astype(jnp.bfloat16)
    lam = lam_ref[...].reshape(n, D)
    full = D // 128 * 128
    main = jnp.dot(perm, lam[:, :full], preferred_element_type=jnp.float32)
    main = main.astype(jnp.bfloat16)
    rest = jnp.dot(perm, lam[:, full:], preferred_element_type=jnp.float32)
    rest = rest.astype(jnp.bfloat16)
    source = lax.broadcasted_iota(jnp.int32, (1024, 1024), 0)
    goal = lax.broadcasted_iota(jnp.int32, (1024, 1024), 1)
    weave = jnp.where(goal == (source % 128) * C_HALF + source // 128, 1.0, 0.0)
    weave = weave.astype(jnp.bfloat16)
    tail = D - full
    source = lax.broadcasted_iota(jnp.int32, (tail, tail * C_HALF), 0)
    goal = lax.broadcasted_iota(jnp.int32, (tail, tail * C_HALF), 1)
    for k, out in enumerate((own_ref, other_ref)):
        first = k * 256
        blocks = [
            jnp.concatenate(
                [
                    main[first + i * ROWS : first + (i + 1) * ROWS, j * 128 : (j + 1) * 128]
                    for i in range(C_HALF)
                ],
                axis=1,
            )
            for j in range(full // 128)
        ]
        woven = jnp.dot(
            jnp.concatenate(blocks, axis=0), weave, preferred_element_type=jnp.float32
        ).astype(jnp.bfloat16)
        for j in range(full // 128):
            out[:, j * 1024 : (j + 1) * 1024] = woven[j * ROWS : (j + 1) * ROWS]
        total = jnp.zeros((ROWS, tail * C_HALF), jnp.float32)
        for i in range(C_HALF):
            put = jnp.where(goal == source * C_HALF + i, 1.0, 0.0).astype(jnp.bfloat16)
            total += jnp.dot(
                rest[first + i * ROWS : first + (i + 1) * ROWS],
                put,
                preferred_element_type=jnp.float32,
            )
        out[:, full * C_HALF :] = total.astype(jnp.bfloat16)


def pack(core, lam):
    piece = jax.ShapeDtypeStruct((ROWS, K_ALL), jnp.bfloat16)
    vmem = pl.BlockSpec(memory_space=pltpu.VMEM)
    return pl.pallas_call(
        pack_kernel,
        out_shape=[piece] * 2,
        in_specs=[pl.BlockSpec(memory_space=pltpu.SMEM), vmem],
        out_specs=[vmem] * 2,
        compiler_params=pltpu.CompilerParams(vmem_limit_bytes=40 * MIB),
        cost_estimate=pl.CostEstimate(
            flops=2 * 512 * 512 * 900, bytes_accessed=2 * MIB, transcendentals=0
        ),
    )(core, lam)


def stage_kernel(in_ref, out_ref):
    pass


def stage(token, *others, cost=10):
    place = pl.BlockSpec(memory_space=pl.ANY)
    return pl.pallas_call(
        stage_kernel,
        out_shape=jax.ShapeDtypeStruct((8, 128), jnp.float32),
        in_specs=[place],
        out_specs=place,
        input_output_aliases={0: 0},
        cost_estimate=pl.CostEstimate(
            flops=cost * 1_000_000_000, bytes_accessed=8192, transcendentals=0
        ),
    )(after(token, *others))


def ladder_kernel(*refs):
    pieces = refs[:-4]
    io_ref, is_ref, po_ref, ps_ref = refs[-4:]
    own, sib = 0.0, 0.0
    for start in range(0, K_ALL, 1024):
        part = slice(start, min(start + 1024, K_ALL))
        lam = jnp.concatenate([piece[:, part] for piece in pieces], axis=0)
        own += jnp.dot(lam, io_ref[part, :], preferred_element_type=jnp.float32)
        sib += jnp.dot(lam, is_ref[part, :], preferred_element_type=jnp.float32)
    po_ref[...] = own
    ps_ref[...] = sib


def ladder(pieces, ints_own, ints_sib):
    m = sum(piece.shape[0] for piece in pieces)
    vmem = pl.BlockSpec(memory_space=pltpu.VMEM)
    out = jax.ShapeDtypeStruct((m, COLS), jnp.float32)
    return pl.pallas_call(
        ladder_kernel,
        out_shape=[out, out],
        in_specs=[vmem] * (len(pieces) + 2),
        out_specs=[vmem] * 2,
        compiler_params=pltpu.CompilerParams(vmem_limit_bytes=40 * MIB),
        cost_estimate=pl.CostEstimate(
            flops=2 * m * K_ALL * 2 * COLS,
            bytes_accessed=2 * K_ALL * (m + 2 * COLS),
            transcendentals=0,
        ),
    )(*pieces, ints_own, ints_sib)


def combine_kernel(spots, place_ref, *refs):
    y, h, core = place_ref[0], place_ref[1], place_ref[2]
    count = len(refs) // 2
    mine, theirs, out_ref = refs[:count], refs[count:-1], refs[-1]
    for (i, sh, sy), (k, row) in spots.items():
        other_k, other_row = spots[1 - i, sh, sy]
        zl = ((h + sh) % 2) * 2 + (core + i) % 2
        out_ref[(y + sy) % 4, zl] = (
            mine[k][row : row + ROWS, :] + theirs[other_k][other_row : other_row + ROWS, :]
        )


def combine(spots, place, mine, theirs):
    vmem = pl.BlockSpec(memory_space=pltpu.VMEM)
    return pl.pallas_call(
        functools.partial(combine_kernel, spots),
        out_shape=jax.ShapeDtypeStruct((4, 4, ROWS, COLS), jnp.float32),
        in_specs=[pl.BlockSpec(memory_space=pltpu.SMEM)] + [vmem] * (2 * len(mine)),
        out_specs=vmem,
        compiler_params=pltpu.CompilerParams(vmem_limit_bytes=16 * MIB),
    )(place, *mine, *theirs)


def spread_kernel(place_ref, t_ref, here_ref, out_ref):
    h = place_ref[1]
    parts = []
    for dh in range(2):
        first = ((h + dh) % 2) * 4
        parts.append(t_ref[first] + t_ref[first + 1] + t_ref[first + 2] + t_ref[first + 3])
    here_ref[...] = parts[0]
    both = jnp.concatenate(parts + [jnp.zeros((2 * ROWS, COLS), jnp.float32)], axis=0)
    row = lax.broadcasted_iota(jnp.int32, (128, COLS), 0)
    col = lax.broadcasted_iota(jnp.int32, (128, COLS), 1)
    target = ((row // 32) * 2 + h) * 2 + (row // 16) % 2
    want = ((row // 4) % 4) * VW + target * 4 + row % 4
    pick = jnp.where(col == want, 1.0, 0.0)
    out_ref[...] = lax.dot_general(
        pick,
        both,
        (((1,), (1,)), ((), ())),
        precision=lax.Precision.HIGHEST,
        preferred_element_type=jnp.float32,
    )


def spread(place, t):
    vmem = pl.BlockSpec(memory_space=pltpu.VMEM)
    return pl.pallas_call(
        spread_kernel,
        out_shape=[
            jax.ShapeDtypeStruct((ROWS, COLS), jnp.float32),
            jax.ShapeDtypeStruct((128, 128), jnp.float32),
        ],
        in_specs=[pl.BlockSpec(memory_space=pltpu.SMEM), vmem],
        out_specs=[vmem] * 2,
        compiler_params=pltpu.CompilerParams(vmem_limit_bytes=16 * MIB),
    )(place, t)


def final_kernel(
    place_ref, t_ref, mine_ref, other_ref, hole_ref, virt_ref, pairs_ref, token_ref, out_ref
):
    h = place_ref[1]
    row = lax.broadcasted_iota(jnp.int32, (128, COLS), 0)
    col = lax.broadcasted_iota(jnp.int32, (128, COLS), 1)
    swapped = jnp.zeros((ROWS, COLS), jnp.float32)
    t = t_ref[...].T
    for dh in range(2):
        source = ((row // 32) * 2 + (h + dh) % 2) * 2 + (row // 16) % 2
        goal = (row % 4) * VW + source * 4 + (row // 4) % 4
        put = jnp.where(col == goal, 1.0, 0.0)
        swapped += jnp.dot(
            t[dh * ROWS : (dh + 1) * ROWS],
            put,
            precision=lax.Precision.HIGHEST,
            preferred_element_type=jnp.float32,
        )
    orbital = lax.broadcasted_iota(jnp.int32, (ROWS, 60), 1)
    holes = jnp.zeros((ROWS, 1), jnp.float32)
    for k in range(2):
        hit = pairs_ref[:, k : k + 1] == orbital
        holes += jnp.sum(jnp.where(hit, hole_ref[...], 0.0), axis=1, keepdims=True)
    denom = holes + virt_ref[...]
    antisym = mine_ref[...] - swapped
    out_ref[...] = -(other_ref[...].astype(jnp.float32) + 0.5 * antisym) / denom


def final(place, t, mine, other_terms, hole, virt, pairs, token):
    vmem = pl.BlockSpec(memory_space=pltpu.VMEM)
    return pl.pallas_call(
        final_kernel,
        out_shape=jax.ShapeDtypeStruct((ROWS, COLS), jnp.float32),
        in_specs=[pl.BlockSpec(memory_space=pltpu.SMEM)] + [vmem] * 7,
        out_specs=vmem,
        compiler_params=pltpu.CompilerParams(vmem_limit_bytes=32 * MIB),
    )(place, t, mine, other_terms, hole, virt, pairs, token)


def group(kind):
    groups = {}
    for p in range(16):
        for q in range(16):
            spot = dict(y=p // 4, h=p // 2 % 2, c=p % 2, x=q // 4, z=q % 4)
            key = tuple(spot[name] for name in "yhcxz" if name not in kind)
            groups.setdefault(key, []).append(p * 16 + q)
    return list(groups.values())


def exchange(value, kind):
    return lax.all_to_all(
        value, ("bulk", "occ"), 0, 0, axis_index_groups=group(kind), tiled=True
    )


def local(lambda_cd, integrals, other_terms, hole_energy, virtual_energy, pair_orbitals):
    p = lax.axis_index("bulk")
    y, h, core = p // 4, (p // 2) % 2, p % 2
    place = jnp.stack([y, h, core]).astype(jnp.int32)

    own, other = pack(core.reshape(1).astype(jnp.int32), lambda_cd)
    shift = bulk_shift
    g = jnp.zeros((8, 128), jnp.float32)
    z0 = shift("z0", own, dh=1)
    sib = shift("sib", other, dc=1)
    r0 = shift("r0", own, dy=-1)
    l0 = shift("l0", own, dy=1)
    g = stage(g, sib, cost=COSTS[0])
    l1 = shift("l1", after(sib, g), dy=1)
    r1 = shift("r1", after(sib, g), dy=-1)
    ints = jnp.transpose(after(integrals, g), (1, 0, 2))
    ints_other = lax.dynamic_slice_in_dim(ints, (1 - core) * C_HALF, C_HALF, axis=1)
    ints_sib = shift("ints", ints_other, dc=1).reshape(K_ALL, COLS)
    g = stage(g, ints_other, cost=COSTS[1])
    z1 = shift("z1", after(sib, g), dh=1)
    g = stage(g, r0, l0, cost=COSTS[2])
    f0 = shift("f0", after(r0, g), dy=-1)
    g = stage(g, r1, l1, cost=COSTS[3])
    f1 = shift("f1", after(l1, g), dy=1)
    g = stage(g, z0, cost=COSTS[4])
    zr0 = shift("zr0", after(z0, g), dy=-1)
    zl0 = shift("zl0", after(z0, g), dy=1)
    ints = jnp.transpose(after(integrals, g), (1, 0, 2))
    ints_own = lax.dynamic_slice_in_dim(ints, core * C_HALF, C_HALF, axis=1)
    ints_own = ints_own.reshape(K_ALL, COLS)
    g = stage(g, z1, f0, f1, cost=COSTS[5])
    zr1 = shift("zr1", after(z1, g), dy=-1)
    zl1 = shift("zl1", after(z1, g), dy=1)
    g = stage(g, zr0, zl0, ints_own, cost=COSTS[6])
    zf0 = shift("zf0", after(zl0, g), dy=1)
    g = stage(g, zr1, cost=COSTS[7])
    zf1 = shift("zf1", after(zr1, g), dy=-1)

    near = {(0, 0, 0): own, (0, 0, 1): r0, (0, 0, 2): f0, (0, 0, 3): l0}
    near |= {(1, 0, 0): sib, (1, 0, 1): r1, (1, 0, 2): f1, (1, 0, 3): l1}
    far = {(0, 1, 0): z0, (0, 1, 1): zr0, (0, 1, 2): zf0, (0, 1, 3): zl0}
    far |= {(1, 1, 0): z1, (1, 1, 1): zr1, (1, 1, 2): zf1, (1, 1, 3): zl1}
    spots, mine, theirs = {}, [], []
    for k, pieces in enumerate((near, far)):
        for n, key in enumerate(pieces):
            spots[key] = (k, n * ROWS)
        po, ps = ladder(tuple(pieces.values()), ints_own, ints_sib)
        mine.append(po)
        theirs.append(shift("t%d" % k, ps, dc=1))
    by_x = combine(spots, place, mine, theirs)
    rows_x = jnp.sum(exchange(by_x, "x"), axis=0)
    by_z = exchange(jnp.concatenate([rows_x, rows_x], axis=0), "hz")
    here, mixed = spread(place, by_z)
    swapped = exchange(mixed.reshape(8, 16, 128), "yc").reshape(128, 128)

    own_virtual = lax.dynamic_slice_in_dim(virtual_energy, p * 4, 4)
    virt = (own_virtual[:, None] + virtual_energy[None, :]).reshape(1, COLS)
    return final(
        place, swapped, here, other_terms, hole_energy.reshape(1, -1), virt, pair_orbitals, g
    )


def solution(mesh):
    placed = (
        P("bulk", "occ", None),
        P("occ", None, "bulk"),
        P("occ", "bulk"),
        P(),
        P(),
        P("occ", None),
    )
    return jax.shard_map(
        local, mesh=mesh, in_specs=placed, out_specs=P("occ", "bulk"), check_vma=False
    )
```

time: 312 us -> 137 us (0.44)
  waiting for transfers between devices: 256 us -> 45.8 us
  starting transfers between devices: 19 us -> 48.4 us
  Pallas kernels: 0 us -> 16.1 us
  matrix products: 15.5 us -> 0 us
  between operations: 13.5 us -> 0.14 us
  blocking collectives: 0 us -> 12.4 us
  local copies, waits for them, and re-layouts: 5.53 us -> 12.5 us
    all_gather x1 -> x0, waiting for transfers between devices: 180 us -> none  [local(): piece = lax.all_gather(lambda_cd, 'bulk', axis=0, tiled=True)]
    reduce_scatter x1 -> x0, waiting for transfers between devices: 67.2 us -> none  [local(): lax.psum_scatter(partial_value, 'occ', scatter_dimension=0, tiled=True)]
    ppermute x0 -> x18, starting transfers between devices: none -> 36.8 us  [bulk_shift(): return lax.ppermute(value, 'bulk', pairs)]
    ppermute x0 -> x18, waiting for transfers between devices: none -> 31.9 us  [bulk_shift(): return lax.ppermute(value, 'bulk', pairs)]
    pallas_call x0 -> x14, Pallas kernels: none -> 16.1 us  [the longest x2 10.4 us: ladder(): pl.pallas_call(ladder_kernel, out_shape=[out, out], in_specs=[vmem] * (le...]
    dot_general x1 -> x0, matrix products: 15.5 us -> none  [local(): jnp.dot(flat_piece, flat_ints, preferred_element_type=jnp.float32)]
    all_to_all x0 -> x1, blocking collectives: none -> 12.4 us  [exchange(): lax.all_to_all(value, ('bulk', 'occ'), 0, 0, axis_index_groups=group(kind...]
    all_to_all x1 -> x2, starting transfers between devices: 19 us -> 11.5 us  [exchange(): lax.all_to_all(value, ('bulk', 'occ'), 0, 0, axis_index_groups=group(kind...]
  transfers between devices with their start and end apart: 3 -> 20, of which waited for: 3 -> 7; matrix products, arithmetic and copies ran while one was open for 0% -> 7% of each run, Pallas kernels for 0% -> 8%
where the time goes in v1:
time: 137 us; the launch traced here: 136 us
  starting transfers between devices  48.4 us (35%)
  waiting for transfers between devices  45.8 us (33%)
  Pallas kernels  16.1 us (12%)
  local copies, waits for them, and re-layouts  12.5 us (9%)
  blocking collectives  12.4 us (9%)
    ppermute x18, starting transfers between devices, bulk_shift(): return lax.ppermute(value, 'bulk', pairs)  36.8 us
    ppermute x18, waiting for transfers between devices, bulk_shift(): return lax.ppermute(value, 'bulk', pairs)  31.9 us
    all_to_all x2, waiting for transfers between devices, exchange(): lax.all_to_all(value, ('bulk', 'occ'), 0, 0, axis_index_groups=group(kind...  13.9 us
    all_to_all x1, blocking collectives, exchange(): lax.all_to_all(value, ('bulk', 'occ'), 0, 0, axis_index_groups=group(kind...  12.4 us
    all_to_all x2, starting transfers between devices, exchange(): lax.all_to_all(value, ('bulk', 'occ'), 0, 0, axis_index_groups=group(kind...  11.5 us
    pallas_call x2, Pallas kernels, ladder(): pl.pallas_call(ladder_kernel, out_shape=[out, out], in_specs=[vmem] * (le...  10.4 us
    reshape x1, local copies, waits for them, and re-layouts, local(): ints_own = ints_own.reshape(K_ALL, COLS)  4.22 us
    dynamic_slice x1, local copies, waits for them, and re-layouts, local(): lax.dynamic_slice_in_dim(ints, (1 - core) * C_HALF, C_HALF, axis=1)  4.11 us
  transfers between devices with their start and end apart: 20, of which 7 were waited for; matrix products, arithmetic and copies ran while one was open for 7% of the time, Pallas kernels for 8%

profile of v1, /device:TPU:1, one launch (start us, length us, event | category | flops | bytes accessed | tf_op | source)
XLA Modules:
  0.0 136.2 jit_solution(11262246380588938339)
XLA Ops:
  0.0 1.2 copy-done.5
  1.2 2.2 %shard_map.64 = (bf16[32,7200]{1,0:T(8,128)(2,1)S(1)}, bf16[32,7200]{1,0:T(8,128)(2,1)S(1)}) custom-call(s32[1]{0:T(128)} %bitcast.2.core_ref, bf16[32,16,900]{2,1,0:T(8,128)(2,1)S(1)} %copy-done.5), custom_call_target="tpu_custom_call" | custom-call | flops 471859200 | bytes 2097152 | tf_op jit(solution)/shard_map/pallas_call | solution.py:89
  3.4 3.3 %collective-permute-start.1 = (bf16[32,7200]{1,0:T(8,128)(2,1)S(1)}, bf16[32,7200]{1,0:T(8,128)(2,1)S(1)}, u32[]{:S(2)}, u32[]{:S(2)}) collective-permute-start(bf16[32,7200]{1,0:T(8,128)(2,1)S(1)} %get-tuple-element.32), channel_id=1, source_target_pairs={{0,16},{16,0},{32,48},{48,32},{64,80},{80,64},{96,112},{112,96},{1... | collective-permute-start | bytes 1382408 | tf_op jit(solution)/shard_map/sib/ppermute | solution.py:31
  6.7 1.0 collective-permute-start
  8.2 6.4 %collective-permute-start.7 = (bf16[32,7200]{1,0:T(8,128)(2,1)S(1)}, bf16[32,7200]{1,0:T(8,128)(2,1)S(1)}, u32[]{:S(2)}, u32[]{:S(2)}) collective-permute-start(bf16[32,7200]{1,0:T(8,128)(2,1)S(1)} %get-tuple-element.31.refs_0_), channel_id=1, source_target_pairs={{0,32},{16,48},{32,0},{48,16},{64,96},{80,112},{96,64},{112,80},{1... | collective-permute-start | bytes 1382408 | tf_op jit(solution)/shard_map/z0/ppermute | solution.py:31
  15.2 2.7 %collective-permute-start.4 = (bf16[32,7200]{1,0:T(8,128)(2,1)S(1)}, bf16[32,7200]{1,0:T(8,128)(2,1)S(1)}, u32[]{:S(2)}, u32[]{:S(2)}) collective-permute-start(bf16[32,7200]{1,0:T(8,128)(2,1)S(1)} %collective-permute-done.1.refs_4_), channel_id=1, source_target_pairs={{0,192},{16,208},{32,224},{48,240},{64,0},{80,16},{96,32},{112,48}... | collective-permute-start | bytes 1382408 | tf_op jit(solution)/shard_map/r1/ppermute | solution.py:31
  17.9 4.1 %dynamic-slice_bitcast_fusion.1 = bf16[900,8,256]{2,1,0:T(8,128)(2,1)} fusion(bf16[16,900,256]{2,0,1:T(8,128)(2,1)} %param.7, s32[]{:T(128)S(6)} %select_n.31), kind=kLoop, calls=%fused_computation.1 | loop fusion | bytes 7372804 | tf_op jit(solution)/shard_map/dynamic_slice | solution.py:280
  22.0 1.2 collective-permute-start.8
  23.2 3.0 %collective-permute-start.3 = (bf16[32,7200]{1,0:T(8,128)(2,1)S(1)}, bf16[32,7200]{1,0:T(8,128)(2,1)}, u32[]{:S(2)}, u32[]{:S(2)}) collective-permute-start(bf16[32,7200]{1,0:T(8,128)(2,1)S(1)} %collective-permute-done.refs_1_), channel_id=1, source_target_pairs={{0,192},{16,208},{32,224},{48,240},{64,0},{80,16},{96,32},{112,48}... | collective-permute-start | bytes 1382408 | tf_op jit(solution)/shard_map/f0/ppermute | solution.py:31
  26.2 2.8 %collective-permute-done.4.refs_5_ = bf16[32,7200]{1,0:T(8,128)(2,1)S(1)} collective-permute-done((bf16[32,7200]{1,0:T(8,128)(2,1)S(1)}, bf16[32,7200]{1,0:T(8,128)(2,1)S(1)}, u32[]{:S(2)}, u32[]{:S(2)}) %collective-permute-start.4) | collective-permute-done | bytes 460832 | tf_op jit(solution)/shard_map/r1/ppermute | solution.py:31
  29.0 5.7 %collective-permute-start.11 = (bf16[32,7200]{1,0:T(8,128)(2,1)S(1)}, bf16[32,7200]{1,0:T(8,128)(2,1)}, u32[]{:S(2)}, u32[]{:S(2)}) collective-permute-start(bf16[32,7200]{1,0:T(8,128)(2,1)S(1)} %collective-permute-done.1.refs_4_), channel_id=1, source_target_pairs={{0,32},{16,48},{32,0},{48,16},{64,96},{80,112},{96,64},{112,80},{1... | collective-permute-start | bytes 1382408 | tf_op jit(solution)/shard_map/z1/ppermute | solution.py:31
  34.7 0.8 collective-permute-start.6
  35.5 2.7 %collective-permute-start.9 = (bf16[32,7200]{1,0:T(8,128)(2,1)S(1)}, bf16[32,7200]{1,0:T(8,128)(2,1)}, u32[]{:S(2)}, u32[]{:S(2)}) collective-permute-start(bf16[32,7200]{1,0:T(8,128)(2,1)S(1)} %collective-permute-done.7.refs_0_), channel_id=1, source_target_pairs={{0,192},{16,208},{32,224},{48,240},{64,0},{80,16},{96,32},{112,48}... | collective-permute-start | bytes 1382408 | tf_op jit(solution)/shard_map/zr0/ppermute | solution.py:31
  38.2 4.2 %dynamic-slice_bitcast_fusion.refs_8_ = bf16[7200,256]{1,0:T(8,128)(2,1)} fusion(bf16[16,900,256]{2,0,1:T(8,128)(2,1)} %param.7, s32[]{:T(128)S(6)} %select_n.32), kind=kLoop, calls=%fused_computation | loop fusion | bytes 7372804 | tf_op jit(solution)/shard_map/reshape | solution.py:293
  42.4 17.6 %collective-permute-done.11.refs_4_ = bf16[32,7200]{1,0:T(8,128)(2,1)} collective-permute-done((bf16[32,7200]{1,0:T(8,128)(2,1)S(1)}, bf16[32,7200]{1,0:T(8,128)(2,1)}, u32[]{:S(2)}, u32[]{:S(2)}) %collective-permute-start.11) | collective-permute-done | bytes 460832 | tf_op jit(solution)/shard_map/z1/ppermute | solution.py:31
  60.0 2.7 %collective-permute-start.13 = (bf16[32,7200]{1,0:T(8,128)(2,1)}, bf16[32,7200]{1,0:T(8,128)(2,1)}, u32[]{:S(2)}, u32[]{:S(2)}) collective-permute-start(bf16[32,7200]{1,0:T(8,128)(2,1)} %collective-permute-done.11.refs_4_), channel_id=1, source_target_pairs={{0,192},{16,208},{32,224},{48,240},{64,0},{80,16},{96,32},{112,48}... | collective-permute-start | bytes 1382408 | tf_op jit(solution)/shard_map/zr1/ppermute | solution.py:31
  62.8 9.8 %collective-permute-done.13.refs_5_ = bf16[32,7200]{1,0:T(8,128)(2,1)} collective-permute-done((bf16[32,7200]{1,0:T(8,128)(2,1)}, bf16[32,7200]{1,0:T(8,128)(2,1)}, u32[]{:S(2)}, u32[]{:S(2)}) %collective-permute-start.13) | collective-permute-done | bytes 460832 | tf_op jit(solution)/shard_map/zr1/ppermute | solution.py:31
  72.6 3.4 %collective-permute-start.14 = (bf16[32,7200]{1,0:T(8,128)(2,1)}, bf16[32,7200]{1,0:T(8,128)(2,1)S(1)}, u32[]{:S(2)}, u32[]{:S(2)}) collective-permute-start(bf16[32,7200]{1,0:T(8,128)(2,1)} %collective-permute-done.13.refs_5_), channel_id=1, source_target_pairs={{0,192},{16,208},{32,224},{48,240},{64,0},{80,16},{96,32},{112,48}... | collective-permute-start | bytes 1382408 | tf_op jit(solution)/shard_map/zf1/ppermute | solution.py:31
  76.0 2.0 %copy-done = bf16[7200,256]{1,0:T(8,128)(2,1)S(1)} copy-done((bf16[7200,256]{1,0:T(8,128)(2,1)S(1)}, bf16[7200,256]{1,0:T(8,128)(2,1)}, u32[]{:S(2)}) %copy-start) | copy-done | bytes 3686424
  78.0 5.3 %shard_map.70 = (f32[256,256]{1,0:T(8,128)S(1)}, f32[256,256]{1,0:T(8,128)}) custom-call(bf16[32,7200]{1,0:T(8,128)(2,1)S(1)} %get-tuple-element.31.refs_0_, bf16[32,7200]{1,0:T(8,128)(2,1)S(1)} %collective-permute-done.refs_1_, bf16[32,7200]{1,0:T(8,128)(2,1)} %collective-permute-done.3.refs_2_, bf16[32,7200]{1,0:T(8,128)(2,1)S(1)} %collective-permute-done.2.refs_3_, ...), custom_call_target="tpu_custom_call" | custom-call | flops 1887436800 | bytes 11059200 | tf_op jit(solution)/shard_map/pallas_call | solution.py:136
  83.4 1.6 %collective-permute-start.16 = (f32[256,256]{1,0:T(8,128)}, f32[256,256]{1,0:T(8,128)S(1)}, u32[]{:S(2)}, u32[]{:S(2)}) collective-permute-start(f32[256,256]{1,0:T(8,128)} %get-tuple-element.53), channel_id=1, source_target_pairs={{0,16},{16,0},{32,48},{48,32},{64,80},{80,64},{96,112},{112,96},{1... | collective-permute-start | bytes 786440 | tf_op jit(solution)/shard_map/t0/ppermute | solution.py:31
  85.7 5.1 %shard_map.74 = (f32[256,256]{1,0:T(8,128)S(1)}, f32[256,256]{1,0:T(8,128)S(1)}) custom-call(bf16[32,7200]{1,0:T(8,128)(2,1)S(1)} %collective-permute-done.7.refs_0_, bf16[32,7200]{1,0:T(8,128)(2,1)} %collective-permute-done.9.refs_1_, bf16[32,7200]{1,0:T(8,128)(2,1)} %collective-permute-done.12.refs_2_, bf16[32,7200]{1,0:T(8,128)(2,1)} %collective-permute-done.10.refs_3_, ...), custom_call_target="tpu_custom_call" | custom-call | flops 1887436800 | bytes 11059200 | tf_op jit(solution)/shard_map/pallas_call | solution.py:136
  90.8 1.7 %collective-permute-start.17 = (f32[256,256]{1,0:T(8,128)S(1)}, f32[256,256]{1,0:T(8,128)S(1)}, u32[]{:S(2)}, u32[]{:S(2)}) collective-permute-start(f32[256,256]{1,0:T(8,128)S(1)} %get-tuple-element.54), channel_id=1, source_target_pairs={{0,16},{16,0},{32,48},{48,32},{64,80},{80,64},{96,112},{112,96},{1... | collective-permute-start | bytes 786440 | tf_op jit(solution)/shard_map/t1/ppermute | solution.py:31
  92.7 1.1 collective-permute-done.17.refs_3_
  94.4 12.4 %all_to_all.15 = f32[4,4,32,256]{3,2,1,0:T(8,128)S(1)} all-to-all(f32[4,4,32,256]{3,2,1,0:T(8,128)S(1)} %shard_map.75), channel_id=1, replica_groups={{0,4,8,12},{1,5,9,13},{2,6,10,14},{3,7,11,15},{16,20,24,28},{17,21,25,2..., dimensions={0} | all-to-all | bytes 1048576 | tf_op jit(solution)/shard_map/all_to_all | solution.py:259
  106.8 0.7 pad_maximum_fusion
  107.5 3.4 %all-to-all-start.1 = ((f32[8,32,256]{2,1,0:T(8,128)}), f32[8,32,256]{2,1,0:T(8,128)S(1)}, u32[]{:S(2)}, u32[]{:S(2)}) async-start(f32[8,32,256]{2,1,0:T(8,128)} %pad_maximum_fusion), calls=%async_computation.1 | async-start | bytes 524288 | tf_op jit(solution)/shard_map/all_to_all | solution.py:259
  111.1 9.3 %all-to-all-done.1.t_ref = f32[8,32,256]{2,1,0:T(8,128)S(1)} async-done(((f32[8,32,256]{2,1,0:T(8,128)}), f32[8,32,256]{2,1,0:T(8,128)S(1)}, u32[]{:S(2)}, u32[]{:S(2)}) %all-to-all-start.1) | async-done | bytes 262176 | tf_op jit(solution)/shard_map/all_to_all | solution.py:259
  120.3 1.5 %shard_map.76 = (f32[32,256]{1,0:T(8,128)S(1)}, f32[128,128]{1,0:T(8,128)}) custom-call(s32[3]{0:T(128)S(1)} %pad_add_fusion.place_ref, f32[8,32,256]{2,1,0:T(8,128)S(1)} %all-to-all-done.1.t_ref), custom_call_target="tpu_custom_call" | custom-call | tf_op jit(solution)/shard_map/pallas_call | solution.py:197
  121.8 8.1 %all-to-all-start.2 = ((f32[8,16,128]{2,1,0:T(8,128)}), f32[8,16,128]{2,1,0:T(8,128)S(1)}, u32[]{:S(2)}, u32[]{:S(2)}) async-start(f32[8,16,128]{2,1,0:T(8,128)} %bitcast.8), calls=%async_computation.2 | async-start | bytes 131072 | tf_op jit(solution)/shard_map/all_to_all | solution.py:259
  130.1 4.6 %all-to-all-done.2 = f32[8,16,128]{2,1,0:T(8,128)S(1)} async-done(((f32[8,16,128]{2,1,0:T(8,128)}), f32[8,16,128]{2,1,0:T(8,128)S(1)}, u32[]{:S(2)}, u32[]{:S(2)}) %all-to-all-start.2) | async-done | bytes 65568 | tf_op jit(solution)/shard_map/all_to_all | solution.py:259
  134.7 1.5 %shard_map.77 = f32[32,256]{1,0:T(8,128)} custom-call(s32[3]{0:T(128)S(1)} %pad_add_fusion.place_ref, f32[128,128]{1,0:T(8,128)S(1)} %bitcast.13, f32[32,256]{1,0:T(8,128)S(1)} %get-tuple-element.56.mine_ref, bf16[32,256]{1,0:T(8,128)(2,1)S(1)} %copy-done.3, f32[1,60]{1,0:T(1,128)S(1)} %bitcast.14, f32[1,256]{1,0:T(1,128)S(1)} %add.49.virt_ref, ...), custom_call_target="tpu_custom_call" | custom-call | tf_op jit(solution)/shard_map/pallas_call | solution.py:239
  (49 shorter events, 3.0 us)
Async XLA Ops:
  0.0 1.2 copy-start.5
  3.4 11.3 %collective-permute-start.1 = (bf16[32,7200]{1,0:T(8,128)(2,1)S(1)}, bf16[32,7200]{1,0:T(8,128)(2,1)S(1)}, u32[]{:S(2)}, u32[]{:S(2)}) collective-permute-start(bf16[32,7200]{1,0:T(8,128)(2,1)S(1)} %get-tuple-element.32), channel_id=1, source_target_pairs={{0,16},{16,0},{32,48},{48,32},{64,80},{80,64},{96,112},{112,96},{1... | collective-permute-start | bytes 1382408 | tf_op jit(solution)/shard_map/sib/ppermute | solution.py:31
  6.7 15.3 %collective-permute-start = (bf16[32,7200]{1,0:T(8,128)(2,1)S(1)}, bf16[32,7200]{1,0:T(8,128)(2,1)S(1)}, u32[]{:S(2)}, u32[]{:S(2)}) collective-permute-start(bf16[32,7200]{1,0:T(8,128)(2,1)S(1)} %get-tuple-element.31.refs_0_), channel_id=1, source_target_pairs={{0,192},{16,208},{32,224},{48,240},{64,0},{80,16},{96,32},{112,48}... | collective-permute-start | bytes 1382408 | tf_op jit(solution)/shard_map/r0/ppermute | solution.py:31
  7.7 15.5 %collective-permute-start.2 = (bf16[32,7200]{1,0:T(8,128)(2,1)S(1)}, bf16[32,7200]{1,0:T(8,128)(2,1)S(1)}, u32[]{:S(2)}, u32[]{:S(2)}) collective-permute-start(bf16[32,7200]{1,0:T(8,128)(2,1)S(1)} %get-tuple-element.31.refs_0_), channel_id=1, source_target_pairs={{0,64},{16,80},{32,96},{48,112},{64,128},{80,144},{96,160},{112,17... | collective-permute-start | bytes 1382408 | tf_op jit(solution)/shard_map/l0/ppermute | solution.py:31
  8.2 27.3 %collective-permute-start.7 = (bf16[32,7200]{1,0:T(8,128)(2,1)S(1)}, bf16[32,7200]{1,0:T(8,128)(2,1)S(1)}, u32[]{:S(2)}, u32[]{:S(2)}) collective-permute-start(bf16[32,7200]{1,0:T(8,128)(2,1)S(1)} %get-tuple-element.31.refs_0_), channel_id=1, source_target_pairs={{0,32},{16,48},{32,0},{48,16},{64,96},{80,112},{96,64},{112,80},{1... | collective-permute-start | bytes 1382408 | tf_op jit(solution)/shard_map/z0/ppermute | solution.py:31
  15.2 13.7 %collective-permute-start.4 = (bf16[32,7200]{1,0:T(8,128)(2,1)S(1)}, bf16[32,7200]{1,0:T(8,128)(2,1)S(1)}, u32[]{:S(2)}, u32[]{:S(2)}) collective-permute-start(bf16[32,7200]{1,0:T(8,128)(2,1)S(1)} %collective-permute-done.1.refs_4_), channel_id=1, source_target_pairs={{0,192},{16,208},{32,224},{48,240},{64,0},{80,16},{96,32},{112,48}... | collective-permute-start | bytes 1382408 | tf_op jit(solution)/shard_map/r1/ppermute | solution.py:31
  17.9 16.8 %collective-permute-start.5 = (bf16[32,7200]{1,0:T(8,128)(2,1)S(1)}, bf16[32,7200]{1,0:T(8,128)(2,1)S(1)}, u32[]{:S(2)}, u32[]{:S(2)}) collective-permute-start(bf16[32,7200]{1,0:T(8,128)(2,1)S(1)} %collective-permute-done.1.refs_4_), channel_id=1, source_target_pairs={{0,64},{16,80},{32,96},{48,112},{64,128},{80,144},{96,160},{112,17... | collective-permute-start | bytes 1382408 | tf_op jit(solution)/shard_map/l1/ppermute | solution.py:31
  22.0 54.0 %collective-permute-start.8 = (bf16[900,8,256]{2,1,0:T(8,128)(2,1)}, bf16[900,8,256]{2,1,0:T(8,128)(2,1)}, u32[]{:S(2)}, u32[]{:S(2)}) collective-permute-start(bf16[900,8,256]{2,1,0:T(8,128)(2,1)} %dynamic-slice_bitcast_fusion.1), channel_id=1, source_target_pairs={{0,16},{16,0},{32,48},{48,32},{64,80},{80,64},{96,112},{112,96},{1... | collective-permute-start | bytes 11059208 | tf_op jit(solution)/shard_map/ints/ppermute | solution.py:31
  23.2 19.2 %collective-permute-start.3 = (bf16[32,7200]{1,0:T(8,128)(2,1)S(1)}, bf16[32,7200]{1,0:T(8,128)(2,1)}, u32[]{:S(2)}, u32[]{:S(2)}) collective-permute-start(bf16[32,7200]{1,0:T(8,128)(2,1)S(1)} %collective-permute-done.refs_1_), channel_id=1, source_target_pairs={{0,192},{16,208},{32,224},{48,240},{64,0},{80,16},{96,32},{112,48}... | collective-permute-start | bytes 1382408 | tf_op jit(solution)/shard_map/f0/ppermute | solution.py:31
  29.0 31.0 %collective-permute-start.11 = (bf16[32,7200]{1,0:T(8,128)(2,1)S(1)}, bf16[32,7200]{1,0:T(8,128)(2,1)}, u32[]{:S(2)}, u32[]{:S(2)}) collective-permute-start(bf16[32,7200]{1,0:T(8,128)(2,1)S(1)} %collective-permute-done.1.refs_4_), channel_id=1, source_target_pairs={{0,32},{16,48},{32,0},{48,16},{64,96},{80,112},{96,64},{112,80},{1... | collective-permute-start | bytes 1382408 | tf_op jit(solution)/shard_map/z1/ppermute | solution.py:31
  34.7 25.3 %collective-permute-start.6 = (bf16[32,7200]{1,0:T(8,128)(2,1)S(1)}, bf16[32,7200]{1,0:T(8,128)(2,1)}, u32[]{:S(2)}, u32[]{:S(2)}) collective-permute-start(bf16[32,7200]{1,0:T(8,128)(2,1)S(1)} %collective-permute-done.5.refs_7_), channel_id=1, source_target_pairs={{0,64},{16,80},{32,96},{48,112},{64,128},{80,144},{96,160},{112,17... | collective-permute-start | bytes 1382408 | tf_op jit(solution)/shard_map/f1/ppermute | solution.py:31
  35.5 27.2 %collective-permute-start.9 = (bf16[32,7200]{1,0:T(8,128)(2,1)S(1)}, bf16[32,7200]{1,0:T(8,128)(2,1)}, u32[]{:S(2)}, u32[]{:S(2)}) collective-permute-start(bf16[32,7200]{1,0:T(8,128)(2,1)S(1)} %collective-permute-done.7.refs_0_), channel_id=1, source_target_pairs={{0,192},{16,208},{32,224},{48,240},{64,0},{80,16},{96,32},{112,48}... | collective-permute-start | bytes 1382408 | tf_op jit(solution)/shard_map/zr0/ppermute | solution.py:31
  42.4 20.3 %collective-permute-start.10 = (bf16[32,7200]{1,0:T(8,128)(2,1)S(1)}, bf16[32,7200]{1,0:T(8,128)(2,1)}, u32[]{:S(2)}, u32[]{:S(2)}) collective-permute-start(bf16[32,7200]{1,0:T(8,128)(2,1)S(1)} %collective-permute-done.7.refs_0_), channel_id=1, source_target_pairs={{0,64},{16,80},{32,96},{48,112},{64,128},{80,144},{96,160},{112,17... | collective-permute-start | bytes 1382408 | tf_op jit(solution)/shard_map/zl0/ppermute | solution.py:31
  60.0 12.6 %collective-permute-start.13 = (bf16[32,7200]{1,0:T(8,128)(2,1)}, bf16[32,7200]{1,0:T(8,128)(2,1)}, u32[]{:S(2)}, u32[]{:S(2)}) collective-permute-start(bf16[32,7200]{1,0:T(8,128)(2,1)} %collective-permute-done.11.refs_4_), channel_id=1, source_target_pairs={{0,192},{16,208},{32,224},{48,240},{64,0},{80,16},{96,32},{112,48}... | collective-permute-start | bytes 1382408 | tf_op jit(solution)/shard_map/zr1/ppermute | solution.py:31
  62.7 23.0 %collective-permute-start.15 = (bf16[32,7200]{1,0:T(8,128)(2,1)}, bf16[32,7200]{1,0:T(8,128)(2,1)}, u32[]{:S(2)}, u32[]{:S(2)}) collective-permute-start(bf16[32,7200]{1,0:T(8,128)(2,1)} %collective-permute-done.11.refs_4_), channel_id=1, source_target_pairs={{0,64},{16,80},{32,96},{48,112},{64,128},{80,144},{96,160},{112,17... | collective-permute-start | bytes 1382408 | tf_op jit(solution)/shard_map/zl1/ppermute | solution.py:31
  62.7 23.0 %collective-permute-start.12 = (bf16[32,7200]{1,0:T(8,128)(2,1)}, bf16[32,7200]{1,0:T(8,128)(2,1)}, u32[]{:S(2)}, u32[]{:S(2)}) collective-permute-start(bf16[32,7200]{1,0:T(8,128)(2,1)} %collective-permute-done.10.refs_3_), channel_id=1, source_target_pairs={{0,64},{16,80},{32,96},{48,112},{64,128},{80,144},{96,160},{112,17... | collective-permute-start | bytes 1382408 | tf_op jit(solution)/shard_map/zf0/ppermute | solution.py:31
  72.6 13.1 %collective-permute-start.14 = (bf16[32,7200]{1,0:T(8,128)(2,1)}, bf16[32,7200]{1,0:T(8,128)(2,1)S(1)}, u32[]{:S(2)}, u32[]{:S(2)}) collective-permute-start(bf16[32,7200]{1,0:T(8,128)(2,1)} %collective-permute-done.13.refs_5_), channel_id=1, source_target_pairs={{0,192},{16,208},{32,224},{48,240},{64,0},{80,16},{96,32},{112,48}... | collective-permute-start | bytes 1382408 | tf_op jit(solution)/shard_map/zf1/ppermute | solution.py:31
  76.0 2.0 %copy-start = (bf16[7200,256]{1,0:T(8,128)(2,1)S(1)}, bf16[7200,256]{1,0:T(8,128)(2,1)}, u32[]{:S(2)}) copy-start(bf16[7200,256]{1,0:T(8,128)(2,1)} %dynamic-slice_bitcast_fusion.refs_8_) | copy-start | bytes 11059204
  78.0 7.6 %copy-start.1 = (bf16[7200,256]{1,0:T(8,128)(2,1)S(1)}, bf16[7200,256]{1,0:T(8,128)(2,1)}, u32[]{:S(2)}) copy-start(bf16[7200,256]{1,0:T(8,128)(2,1)} %dynamic-slice_bitcast_fusion.refs_8_) | copy-start | bytes 11059204
  83.4 9.3 %collective-permute-start.16 = (f32[256,256]{1,0:T(8,128)}, f32[256,256]{1,0:T(8,128)S(1)}, u32[]{:S(2)}, u32[]{:S(2)}) collective-permute-start(f32[256,256]{1,0:T(8,128)} %get-tuple-element.53), channel_id=1, source_target_pairs={{0,16},{16,0},{32,48},{48,32},{64,80},{80,64},{96,112},{112,96},{1... | collective-permute-start | bytes 786440 | tf_op jit(solution)/shard_map/t0/ppermute | solution.py:31
  90.8 20.2 %copy-start.7 = (f32[64]{0:T(128)S(1)}, f32[64]{0:T(128)}, u32[]{:S(2)}) copy-start(f32[64]{0:T(128)} %param.10) | copy-start | bytes 772
  90.8 39.3 %copy-start.6 = (s32[32,2]{0,1:T(2,128)S(1)}, s32[32,2]{0,1:T(2,128)}, u32[]{:S(2)}) copy-start(s32[32,2]{0,1:T(2,128)} %param.11) | copy-start | bytes 772
  90.8 44.0 %copy-start.2 = (f32[8,128]{1,0:T(8,128)S(1)}, f32[8,128]{1,0:T(8,128)}, u32[]{:S(2)}) copy-start(f32[8,128]{1,0:T(8,128)} %shard_map.73.token_ref) | copy-start | bytes 12292
  90.8 43.9 %copy-start.3 = (bf16[32,256]{1,0:T(8,128)(2,1)S(1)}, bf16[32,256]{1,0:T(8,128)(2,1)}, u32[]{:S(2)}) copy-start(bf16[32,256]{1,0:T(8,128)(2,1)} %other_ref.1) | copy-start | bytes 49156
  90.8 43.9 %copy-start.4 = (f32[60]{0:T(128)S(1)}, f32[60]{0:T(128)}, u32[]{:S(2)}) copy-start(f32[60]{0:T(128)} %param.9) | copy-start | bytes 724
  90.8 2.9 %collective-permute-start.17 = (f32[256,256]{1,0:T(8,128)S(1)}, f32[256,256]{1,0:T(8,128)S(1)}, u32[]{:S(2)}, u32[]{:S(2)}) collective-permute-start(f32[256,256]{1,0:T(8,128)S(1)} %get-tuple-element.54), channel_id=1, source_target_pairs={{0,16},{16,0},{32,48},{48,32},{64,80},{80,64},{96,112},{112,96},{1... | collective-permute-start | bytes 786440 | tf_op jit(solution)/shard_map/t1/ppermute | solution.py:31
  107.5 12.8 %all-to-all-start.1 = ((f32[8,32,256]{2,1,0:T(8,128)}), f32[8,32,256]{2,1,0:T(8,128)S(1)}, u32[]{:S(2)}, u32[]{:S(2)}) async-start(f32[8,32,256]{2,1,0:T(8,128)} %pad_maximum_fusion), calls=%async_computation.1 | async-start | bytes 524288 | tf_op jit(solution)/shard_map/all_to_all | solution.py:259
  121.8 13.0 %all-to-all-start.2 = ((f32[8,16,128]{2,1,0:T(8,128)}), f32[8,16,128]{2,1,0:T(8,128)S(1)}, u32[]{:S(2)}, u32[]{:S(2)}) async-start(f32[8,16,128]{2,1,0:T(8,128)} %bitcast.8), calls=%async_computation.2 | async-start | bytes 131072 | tf_op jit(solution)/shard_map/all_to_all | solution.py:259

commit v2 on v1

--- a/solution.py
+++ b/solution.py
@@ -10,6 +10,7 @@
 VW = 64
 COLS = 256
 ROWS = 32
+HALF = 16
 C_HALF = 8
 D = 900
 K_ALL = C_HALF * D
@@ -19,6 +20,11 @@
 
 def p_of(y, h, core):
     return ((y % 4) * 2 + h % 2) * 2 + core % 2
+
+
+def here():
+    p = lax.axis_index("bulk")
+    return p // 4, (p // 2) % 2, p % 2
 
 
 def bulk_shift(name, value, dy=0, dh=0, dc=0):
@@ -35,8 +41,9 @@
     return lax.optimization_barrier((value,) + others)[0]
 
 
-def pack_kernel(core_ref, lam_ref, own_ref, other_ref):
-    core = core_ref[0]
+def pack_kernel(lam_ref, own_ref, other_ref, token_ref):
+    _, _, core = here()
+    token_ref[...] = jnp.zeros_like(token_ref)
     n = ROWS * 16
     row = lax.broadcasted_iota(jnp.int32, (n, n), 0)
     col = lax.broadcasted_iota(jnp.int32, (n, n), 1)
@@ -83,19 +90,19 @@
         out[:, full * C_HALF :] = total.astype(jnp.bfloat16)
 
 
-def pack(core, lam):
+def pack(lam):
     piece = jax.ShapeDtypeStruct((ROWS, K_ALL), jnp.bfloat16)
     vmem = pl.BlockSpec(memory_space=pltpu.VMEM)
     return pl.pallas_call(
         pack_kernel,
-        out_shape=[piece] * 2,
-        in_specs=[pl.BlockSpec(memory_space=pltpu.SMEM), vmem],
-        out_specs=[vmem] * 2,
-        compiler_params=pltpu.CompilerParams(vmem_limit_bytes=40 * MIB),
+        out_shape=[piece, piece, jax.ShapeDtypeStruct((8, 128), jnp.float32)],
+        in_specs=[vmem],
+        out_specs=[vmem] * 3,
+        compiler_params=pltpu.CompilerParams(vmem_limit_bytes=24 * MIB),
         cost_estimate=pl.CostEstimate(
             flops=2 * 512 * 512 * 900, bytes_accessed=2 * MIB, transcendentals=0
         ),
-    )(core, lam)
+    )(lam)
 
 
 def stage_kernel(in_ref, out_ref):
@@ -110,6 +117,7 @@
         in_specs=[place],
         out_specs=place,
         input_output_aliases={0: 0},
+        compiler_params=pltpu.CompilerParams(vmem_limit_bytes=MIB // 4),
         cost_estimate=pl.CostEstimate(
             flops=cost * 1_000_000_000, bytes_accessed=8192, transcendentals=0
         ),
@@ -117,38 +125,35 @@
 
 
 def ladder_kernel(*refs):
-    pieces = refs[:-4]
-    io_ref, is_ref, po_ref, ps_ref = refs[-4:]
-    own, sib = 0.0, 0.0
+    pieces = refs[:-2]
+    ints_ref, out_ref = refs[-2:]
+    total = 0.0
     for start in range(0, K_ALL, 1024):
         part = slice(start, min(start + 1024, K_ALL))
         lam = jnp.concatenate([piece[:, part] for piece in pieces], axis=0)
-        own += jnp.dot(lam, io_ref[part, :], preferred_element_type=jnp.float32)
-        sib += jnp.dot(lam, is_ref[part, :], preferred_element_type=jnp.float32)
-    po_ref[...] = own
-    ps_ref[...] = sib
-
-
-def ladder(pieces, ints_own, ints_sib):
+        total += jnp.dot(lam, ints_ref[part, :], preferred_element_type=jnp.float32)
+    out_ref[...] = total
+
+
+def ladder(pieces, ints):
     m = sum(piece.shape[0] for piece in pieces)
     vmem = pl.BlockSpec(memory_space=pltpu.VMEM)
-    out = jax.ShapeDtypeStruct((m, COLS), jnp.float32)
     return pl.pallas_call(
         ladder_kernel,
-        out_shape=[out, out],
-        in_specs=[vmem] * (len(pieces) + 2),
-        out_specs=[vmem] * 2,
-        compiler_params=pltpu.CompilerParams(vmem_limit_bytes=40 * MIB),
+        out_shape=jax.ShapeDtypeStruct((m, COLS), jnp.float32),
+        in_specs=[vmem] * (len(pieces) + 1),
+        out_specs=vmem,
+        compiler_params=pltpu.CompilerParams(vmem_limit_bytes=16 * MIB),
         cost_estimate=pl.CostEstimate(
-            flops=2 * m * K_ALL * 2 * COLS,
-            bytes_accessed=2 * K_ALL * (m + 2 * COLS),
+            flops=2 * m * K_ALL * COLS,
+            bytes_accessed=2 * K_ALL * (m + COLS),
             transcendentals=0,
         ),
-    )(*pieces, ints_own, ints_sib)
-
-
-def combine_kernel(spots, place_ref, *refs):
-    y, h, core = place_ref[0], place_ref[1], place_ref[2]
+    )(*pieces, ints)
+
+
+def combine_kernel(spots, *refs):
+    y, h, core = here()
     count = len(refs) // 2
     mine, theirs, out_ref = refs[:count], refs[count:-1], refs[-1]
     for (i, sh, sy), (k, row) in spots.items():
@@ -159,19 +164,19 @@
         )
 
 
-def combine(spots, place, mine, theirs):
+def combine(spots, mine, theirs):
     vmem = pl.BlockSpec(memory_space=pltpu.VMEM)
     return pl.pallas_call(
         functools.partial(combine_kernel, spots),
         out_shape=jax.ShapeDtypeStruct((4, 4, ROWS, COLS), jnp.float32),
-        in_specs=[pl.BlockSpec(memory_space=pltpu.SMEM)] + [vmem] * (2 * len(mine)),
+        in_specs=[vmem] * (2 * len(mine)),
         out_specs=vmem,
-        compiler_params=pltpu.CompilerParams(vmem_limit_bytes=16 * MIB),
-    )(place, *mine, *theirs)
-
-
-def spread_kernel(place_ref, t_ref, here_ref, out_ref):
-    h = place_ref[1]
+        compiler_params=pltpu.CompilerParams(vmem_limit_bytes=8 * MIB),
+    )(*mine, *theirs)
+
+
+def spread_kernel(t_ref, here_ref, out_ref):
+    _, h, _ = here()
     parts = []
     for dh in range(2):
         first = ((h + dh) % 2) * 4
@@ -192,7 +197,7 @@
     )
 
 
-def spread(place, t):
+def spread(t):
     vmem = pl.BlockSpec(memory_space=pltpu.VMEM)
     return pl.pallas_call(
         spread_kernel,
@@ -200,16 +205,15 @@
             jax.ShapeDtypeStruct((ROWS, COLS), jnp.float32),
             jax.ShapeDtypeStruct((128, 128), jnp.float32),
         ],
-        in_specs=[pl.BlockSpec(memory_space=pltpu.SMEM), vmem],
+        in_specs=[vmem],
         out_specs=[vmem] * 2,
-        compiler_params=pltpu.CompilerParams(vmem_limit_bytes=16 * MIB),
-    )(place, t)
-
-
-def final_kernel(
-    place_ref, t_ref, mine_ref, other_ref, hole_ref, virt_ref, pairs_ref, token_ref, out_ref
-):
-    h = place_ref[1]
+        compiler_params=pltpu.CompilerParams(vmem_limit_bytes=8 * MIB),
+    )(t)
+
+
+def final_kernel(t_ref, mine_ref, other_ref, hole_ref, virt_ref, pairs_ref, token_ref, out_ref):
+    y, h, core = here()
+    exact = dict(precision=lax.Precision.HIGHEST, preferred_element_type=jnp.float32)
     row = lax.broadcasted_iota(jnp.int32, (128, COLS), 0)
     col = lax.broadcasted_iota(jnp.int32, (128, COLS), 1)
     swapped = jnp.zeros((ROWS, COLS), jnp.float32)
@@ -218,31 +222,38 @@
         source = ((row // 32) * 2 + (h + dh) % 2) * 2 + (row // 16) % 2
         goal = (row % 4) * VW + source * 4 + (row // 4) % 4
         put = jnp.where(col == goal, 1.0, 0.0)
-        swapped += jnp.dot(
-            t[dh * ROWS : (dh + 1) * ROWS],
-            put,
-            precision=lax.Precision.HIGHEST,
-            preferred_element_type=jnp.float32,
-        )
-    orbital = lax.broadcasted_iota(jnp.int32, (ROWS, 60), 1)
+        swapped += jnp.dot(t[dh * ROWS : (dh + 1) * ROWS], put, **exact)
+    own_a = ((y * 2 + h) * 2 + core) * 4 + col[:VW] // VW
+    pick_a = jnp.where(row[:VW] == own_a, 1.0, 0.0)
+    pick_b = jnp.where(row[:VW] == col[:VW] % VW, 1.0, 0.0)
+    virtual = jnp.broadcast_to(virt_ref[...], (8, VW))
+    virt_a = jnp.dot(virtual, pick_a, **exact)[:1]
+    virt_b = jnp.dot(virtual, pick_b, **exact)[:1]
+    count = hole_ref.shape[1]
+    orbital = lax.broadcasted_iota(jnp.int32, (count, ROWS), 0)
+    hole = jnp.broadcast_to(hole_ref[...], (8, count))
+    diagonal = lax.broadcasted_iota(jnp.int32, (ROWS, ROWS), 0) == lax.broadcasted_iota(
+        jnp.int32, (ROWS, ROWS), 1
+    )
     holes = jnp.zeros((ROWS, 1), jnp.float32)
     for k in range(2):
-        hit = pairs_ref[:, k : k + 1] == orbital
-        holes += jnp.sum(jnp.where(hit, hole_ref[...], 0.0), axis=1, keepdims=True)
-    denom = holes + virt_ref[...]
+        pick = jnp.where(orbital == pairs_ref[k : k + 1, :], 1.0, 0.0)
+        energy = jnp.dot(hole, pick, **exact)[:1]
+        holes += jnp.sum(jnp.where(diagonal, energy, 0.0), axis=1, keepdims=True)
+    denom = holes + virt_a + virt_b
     antisym = mine_ref[...] - swapped
     out_ref[...] = -(other_ref[...].astype(jnp.float32) + 0.5 * antisym) / denom
 
 
-def final(place, t, mine, other_terms, hole, virt, pairs, token):
+def final(t, mine, other_terms, hole, virt, pairs, token):
     vmem = pl.BlockSpec(memory_space=pltpu.VMEM)
     return pl.pallas_call(
         final_kernel,
         out_shape=jax.ShapeDtypeStruct((ROWS, COLS), jnp.float32),
-        in_specs=[pl.BlockSpec(memory_space=pltpu.SMEM)] + [vmem] * 7,
+        in_specs=[vmem] * 6 + [pl.BlockSpec(memory_space=pl.ANY)],
         out_specs=vmem,
-        compiler_params=pltpu.CompilerParams(vmem_limit_bytes=32 * MIB),
-    )(place, t, mine, other_terms, hole, virt, pairs, token)
+        compiler_params=pltpu.CompilerParams(vmem_limit_bytes=8 * MIB),
+    )(t, mine, other_terms, hole, virt, pairs, token)
 
 
 def group(kind):
@@ -262,13 +273,9 @@
 
 
 def local(lambda_cd, integrals, other_terms, hole_energy, virtual_energy, pair_orbitals):
-    p = lax.axis_index("bulk")
-    y, h, core = p // 4, (p // 2) % 2, p % 2
-    place = jnp.stack([y, h, core]).astype(jnp.int32)
-
-    own, other = pack(core.reshape(1).astype(jnp.int32), lambda_cd)
+    core = lax.axis_index("bulk") % 2
+    own, other, g = pack(lambda_cd)
     shift = bulk_shift
-    g = jnp.zeros((8, 128), jnp.float32)
     z0 = shift("z0", own, dh=1)
     sib = shift("sib", other, dc=1)
     r0 = shift("r0", own, dy=-1)
@@ -307,19 +314,25 @@
     for k, pieces in enumerate((near, far)):
         for n, key in enumerate(pieces):
             spots[key] = (k, n * ROWS)
-        po, ps = ladder(tuple(pieces.values()), ints_own, ints_sib)
-        mine.append(po)
-        theirs.append(shift("t%d" % k, ps, dc=1))
-    by_x = combine(spots, place, mine, theirs)
+        pieces = jax.tree.leaves(list(pieces.values()))
+        part = ladder(pieces, after(ints_sib, *mine, *theirs))
+        theirs.append(shift("t%d" % k, part, dc=1))
+        mine.append(ladder(pieces, after(ints_own, part)))
+    by_x = combine(spots, mine, theirs)
     rows_x = jnp.sum(exchange(by_x, "x"), axis=0)
-    by_z = exchange(jnp.concatenate([rows_x, rows_x], axis=0), "hz")
-    here, mixed = spread(place, by_z)
+    by_z = jnp.broadcast_to(rows_x[None], (2,) + rows_x.shape).reshape(8, ROWS, COLS)
+    by_z = exchange(by_z, "hz")
+    direct, mixed = spread(by_z)
     swapped = exchange(mixed.reshape(8, 16, 128), "yc").reshape(128, 128)
 
-    own_virtual = lax.dynamic_slice_in_dim(virtual_energy, p * 4, 4)
-    virt = (own_virtual[:, None] + virtual_energy[None, :]).reshape(1, COLS)
     return final(
-        place, swapped, here, other_terms, hole_energy.reshape(1, -1), virt, pair_orbitals, g
+        swapped,
+        direct,
+        other_terms,
+        hole_energy.reshape(1, -1),
+        virtual_energy.reshape(1, -1),
+        pair_orbitals.T,
+        g,
     )
 
 

time: 137 us -> 129 us (0.942)
  blocking collectives: 12.4 us -> 37.2 us
  waiting for transfers between devices: 45.8 us -> 36.1 us
  Pallas kernels: 16.1 us -> 8.43 us
  local copies, waits for them, and re-layouts: 12.5 us -> 4.85 us
  starting transfers between devices: 48.4 us -> 41.4 us
    all_to_all x1 -> x3, blocking collectives: 12.4 us -> 37.2 us  [exchange(): lax.all_to_all(value, ('bulk', 'occ'), 0, 0, axis_index_groups=group(kind...]
    all_to_all x2 -> x0, waiting for transfers between devices: 13.9 us -> none  [exchange(): lax.all_to_all(value, ('bulk', 'occ'), 0, 0, axis_index_groups=group(kind...]
    all_to_all x2 -> x0, starting transfers between devices: 11.5 us -> none  [exchange(): lax.all_to_all(value, ('bulk', 'occ'), 0, 0, axis_index_groups=group(kind...]
    pallas_call x3 -> x5, Pallas kernels: 12.6 us -> 6.94 us  [the longest x4 4.77 us: ladder(): pl.pallas_call(ladder_kernel, out_shape=jax.ShapeDtypeStruct((m, COLS), j...]
    ppermute x18, starting transfers between devices: 36.8 us -> 41.4 us  [bulk_shift(): return lax.ppermute(value, 'bulk', pairs)]
    ppermute x18, waiting for transfers between devices: 31.9 us -> 36.1 us  [bulk_shift(): return lax.ppermute(value, 'bulk', pairs)]
    reshape x1, local copies, waits for them, and re-layouts: 4.22 us -> 0.25 us  [local(): ints_own = ints_own.reshape(K_ALL, COLS)]
    dynamic_slice x1, local copies, waits for them, and re-layouts: 4.11 us -> 0.24 us  [local(): lax.dynamic_slice_in_dim(ints, (1 - core) * C_HALF, C_HALF, axis=1)]
  transfers between devices with their start and end apart: 20 -> 18, of which waited for: 7 -> 5; matrix products, arithmetic and copies ran while one was open for 7% -> 0% of each run, Pallas kernels for 8% -> 3%
where the time goes in v2:
time: 129 us; the launch traced here: 128 us
  starting transfers between devices  41.4 us (32%)
  blocking collectives  37.2 us (29%)
  waiting for transfers between devices  36.1 us (28%)
  Pallas kernels  8.43 us (7%)
  local copies, waits for them, and re-layouts  4.85 us (4%)
    ppermute x18, starting transfers between devices, bulk_shift(): return lax.ppermute(value, 'bulk', pairs)  41.4 us
    all_to_all x3, blocking collectives, exchange(): lax.all_to_all(value, ('bulk', 'occ'), 0, 0, axis_index_groups=group(kind...  37.2 us
    ppermute x18, waiting for transfers between devices, bulk_shift(): return lax.ppermute(value, 'bulk', pairs)  36.1 us
    pallas_call x4, Pallas kernels, ladder(): pl.pallas_call(ladder_kernel, out_shape=jax.ShapeDtypeStruct((m, COLS), j...  4.77 us
    unnamed x12, local copies, waits for them, and re-layouts  4.34 us
  transfers between devices with their start and end apart: 18, of which 5 were waited for; matrix products, arithmetic and copies ran while one was open for 0% of the time, Pallas kernels for 3%

profile of v2, /device:TPU:1, one launch (start us, length us, event | category | flops | bytes accessed | tf_op | source)
XLA Modules:
  0.0 128.3 jit_solution(8251393515221240395)
XLA Ops:
  0.0 1.2 copy-done.4
  1.2 2.2 %shard_map.64 = (bf16[32,7200]{1,0:T(8,128)(2,1)S(1)}, bf16[32,7200]{1,0:T(8,128)(2,1)S(1)}, f32[8,128]{1,0:T(8,128)S(1)}) custom-call(bf16[32,16,900]{2,1,0:T(8,128)(2,1)S(1)} %copy-done.4), custom_call_target="tpu_custom_call" | custom-call | flops 471859200 | bytes 2097152 | tf_op jit(solution)/shard_map/pallas_call | solution.py:96
  3.4 3.3 %collective-permute-start.1 = (bf16[32,7200]{1,0:T(8,128)(2,1)S(1)}, bf16[32,7200]{1,0:T(8,128)(2,1)S(1)}, u32[]{:S(2)}, u32[]{:S(2)}) collective-permute-start(bf16[32,7200]{1,0:T(8,128)(2,1)S(1)} %get-tuple-element.33), channel_id=1, source_target_pairs={{0,16},{16,0},{32,48},{48,32},{64,80},{80,64},{96,112},{112,96},{1... | collective-permute-start | bytes 1382408 | tf_op jit(solution)/shard_map/sib/ppermute | solution.py:37
  6.7 1.0 collective-permute-start
  7.7 0.5 collective-permute-start.2
  8.2 6.4 %collective-permute-start.7 = (bf16[32,7200]{1,0:T(8,128)(2,1)S(1)}, bf16[32,7200]{1,0:T(8,128)(2,1)S(1)}, u32[]{:S(2)}, u32[]{:S(2)}) collective-permute-start(bf16[32,7200]{1,0:T(8,128)(2,1)S(1)} %get-tuple-element.31.refs_0_), channel_id=1, source_target_pairs={{0,32},{16,48},{32,0},{48,16},{64,96},{80,112},{96,64},{112,80},{1... | collective-permute-start | bytes 1382408 | tf_op jit(solution)/shard_map/z0/ppermute | solution.py:37
  14.7 3.1 %copy-done.5 = bf16[16,900,256]{2,0,1:T(8,128)(2,1)S(1)} copy-done((bf16[16,900,256]{2,0,1:T(8,128)(2,1)S(1)}, bf16[16,900,256]{2,0,1:T(8,128)(2,1)}, u32[]{:S(2)}) %copy-start.5) | copy-done | bytes 7372824
  18.0 0.7 collective-permute-start.8
  18.7 0.3 collective-permute-start.5
  19.1 2.6 %collective-permute-start.4 = (bf16[32,7200]{1,0:T(8,128)(2,1)S(1)}, bf16[32,7200]{1,0:T(8,128)(2,1)S(1)}, u32[]{:S(2)}, u32[]{:S(2)}) collective-permute-start(bf16[32,7200]{1,0:T(8,128)(2,1)S(1)} %collective-permute-done.1.refs_4_), channel_id=1, source_target_pairs={{0,192},{16,208},{32,224},{48,240},{64,0},{80,16},{96,32},{112,48}... | collective-permute-start | bytes 1382408 | tf_op jit(solution)/shard_map/r1/ppermute | solution.py:37
  21.7 1.5 %collective-permute-start.3 = (bf16[32,7200]{1,0:T(8,128)(2,1)S(1)}, bf16[32,7200]{1,0:T(8,128)(2,1)S(1)}, u32[]{:S(2)}, u32[]{:S(2)}) collective-permute-start(bf16[32,7200]{1,0:T(8,128)(2,1)S(1)} %collective-permute-done.refs_1_), channel_id=1, source_target_pairs={{0,192},{16,208},{32,224},{48,240},{64,0},{80,16},{96,32},{112,48}... | collective-permute-start | bytes 1382408 | tf_op jit(solution)/shard_map/f0/ppermute | solution.py:37
  23.2 9.5 %collective-permute-done.5.refs_7_ = bf16[32,7200]{1,0:T(8,128)(2,1)S(1)} collective-permute-done((bf16[32,7200]{1,0:T(8,128)(2,1)S(1)}, bf16[32,7200]{1,0:T(8,128)(2,1)S(1)}, u32[]{:S(2)}, u32[]{:S(2)}) %collective-permute-start.5) | collective-permute-done | bytes 460832 | tf_op jit(solution)/shard_map/l1/ppermute | solution.py:37
  32.6 5.1 %collective-permute-start.11 = (bf16[32,7200]{1,0:T(8,128)(2,1)S(1)}, bf16[32,7200]{1,0:T(8,128)(2,1)S(1)}, u32[]{:S(2)}, u32[]{:S(2)}) collective-permute-start(bf16[32,7200]{1,0:T(8,128)(2,1)S(1)} %collective-permute-done.1.refs_4_), channel_id=1, source_target_pairs={{0,32},{16,48},{32,0},{48,16},{64,96},{80,112},{96,64},{112,80},{1... | collective-permute-start | bytes 1382408 | tf_op jit(solution)/shard_map/z1/ppermute | solution.py:37
  37.9 0.2 dynamic-slice_bitcast_fusion.refs_8_
  38.2 3.2 %collective-permute-done.3.refs_2_ = bf16[32,7200]{1,0:T(8,128)(2,1)S(1)} collective-permute-done((bf16[32,7200]{1,0:T(8,128)(2,1)S(1)}, bf16[32,7200]{1,0:T(8,128)(2,1)S(1)}, u32[]{:S(2)}, u32[]{:S(2)}) %collective-permute-start.3) | collective-permute-done | bytes 460832 | tf_op jit(solution)/shard_map/f0/ppermute | solution.py:37
  41.4 3.4 %collective-permute-start.9 = (bf16[32,7200]{1,0:T(8,128)(2,1)S(1)}, bf16[32,7200]{1,0:T(8,128)(2,1)S(1)}, u32[]{:S(2)}, u32[]{:S(2)}) collective-permute-start(bf16[32,7200]{1,0:T(8,128)(2,1)S(1)} %collective-permute-done.7.refs_0_), channel_id=1, source_target_pairs={{0,192},{16,208},{32,224},{48,240},{64,0},{80,16},{96,32},{112,48}... | collective-permute-start | bytes 1382408 | tf_op jit(solution)/shard_map/zr0/ppermute | solution.py:37
  44.8 8.4 %collective-permute-done.11.refs_4_ = bf16[32,7200]{1,0:T(8,128)(2,1)S(1)} collective-permute-done((bf16[32,7200]{1,0:T(8,128)(2,1)S(1)}, bf16[32,7200]{1,0:T(8,128)(2,1)S(1)}, u32[]{:S(2)}, u32[]{:S(2)}) %collective-permute-start.11) | collective-permute-done | bytes 460832 | tf_op jit(solution)/shard_map/z1/ppermute | solution.py:37
  53.2 9.4 %collective-permute-start.13 = (bf16[32,7200]{1,0:T(8,128)(2,1)S(1)}, bf16[32,7200]{1,0:T(8,128)(2,1)S(1)}, u32[]{:S(2)}, u32[]{:S(2)}) collective-permute-start(bf16[32,7200]{1,0:T(8,128)(2,1)S(1)} %collective-permute-done.11.refs_4_), channel_id=1, source_target_pairs={{0,192},{16,208},{32,224},{48,240},{64,0},{80,16},{96,32},{112,48}... | collective-permute-start | bytes 1382408 | tf_op jit(solution)/shard_map/zr1/ppermute | solution.py:37
  62.7 9.5 %collective-permute-done.13.refs_5_ = bf16[32,7200]{1,0:T(8,128)(2,1)S(1)} collective-permute-done((bf16[32,7200]{1,0:T(8,128)(2,1)S(1)}, bf16[32,7200]{1,0:T(8,128)(2,1)S(1)}, u32[]{:S(2)}, u32[]{:S(2)}) %collective-permute-start.13) | collective-permute-done | bytes 460832 | tf_op jit(solution)/shard_map/zr1/ppermute | solution.py:37
  72.2 3.4 %collective-permute-start.14 = (bf16[32,7200]{1,0:T(8,128)(2,1)S(1)}, bf16[32,7200]{1,0:T(8,128)(2,1)S(1)}, u32[]{:S(2)}, u32[]{:S(2)}) collective-permute-start(bf16[32,7200]{1,0:T(8,128)(2,1)S(1)} %collective-permute-done.13.refs_5_), channel_id=1, source_target_pairs={{0,192},{16,208},{32,224},{48,240},{64,0},{80,16},{96,32},{112,48}... | collective-permute-start | bytes 1382408 | tf_op jit(solution)/shard_map/zf1/ppermute | solution.py:37
  75.6 1.2 shard_map.70
  76.8 1.7 %collective-permute-start.16 = (f32[256,256]{1,0:T(8,128)S(1)}, f32[256,256]{1,0:T(8,128)S(1)}, u32[]{:S(2)}, u32[]{:S(2)}) collective-permute-start(f32[256,256]{1,0:T(8,128)S(1)} %shard_map.70), channel_id=1, source_target_pairs={{0,16},{16,0},{32,48},{48,32},{64,80},{80,64},{96,112},{112,96},{1... | collective-permute-start | bytes 786440 | tf_op jit(solution)/shard_map/t0/ppermute | solution.py:37
  78.5 1.2 shard_map.71.refs_0_
  79.7 5.5 %collective-permute-done.12.refs_2_ = bf16[32,7200]{1,0:T(8,128)(2,1)S(1)} collective-permute-done((bf16[32,7200]{1,0:T(8,128)(2,1)S(1)}, bf16[32,7200]{1,0:T(8,128)(2,1)S(1)}, u32[]{:S(2)}, u32[]{:S(2)}) %collective-permute-start.12) | collective-permute-done | bytes 460832 | tf_op jit(solution)/shard_map/zf0/ppermute | solution.py:37
  85.3 1.2 shard_map.75
  86.5 1.8 %collective-permute-start.17 = (f32[256,256]{1,0:T(8,128)S(1)}, f32[256,256]{1,0:T(8,128)S(1)}, u32[]{:S(2)}, u32[]{:S(2)}) collective-permute-start(f32[256,256]{1,0:T(8,128)S(1)} %shard_map.75), channel_id=1, source_target_pairs={{0,16},{16,0},{32,48},{48,32},{64,80},{80,64},{96,112},{112,96},{1... | collective-permute-start | bytes 786440 | tf_op jit(solution)/shard_map/t1/ppermute | solution.py:37
  88.2 1.2 shard_map.76.refs_1_
  89.6 12.8 %all_to_all.15 = f32[4,4,32,256]{3,2,1,0:T(8,128)S(1)} all-to-all(f32[4,4,32,256]{3,2,1,0:T(8,128)S(1)} %shard_map.77), channel_id=1, replica_groups={{0,4,8,12},{1,5,9,13},{2,6,10,14},{3,7,11,15},{16,20,24,28},{17,21,25,2..., dimensions={0} | all-to-all | bytes 1048576 | tf_op jit(solution)/shard_map/all_to_all | solution.py:270
  102.4 12.5 %all_to_all.16.t_ref = f32[8,32,256]{2,1,0:T(8,128)S(1)} all-to-all(f32[8,32,256]{2,1,0:T(8,128)S(1)} %bitcast.20), channel_id=1, replica_groups={{0,1,2,3,32,33,34,35},{4,5,6,7,36,37,38,39},{8,9,10,11,40,41,42,43},{12..., dimensions={0} | all-to-all | bytes 524288 | tf_op jit(solution)/shard_map/all_to_all | solution.py:270
  114.9 0.3 shard_map.78
  115.2 11.9 %all_to_all.17 = f32[8,16,128]{2,1,0:T(8,128)S(1)} all-to-all(f32[8,16,128]{2,1,0:T(8,128)S(1)} %bitcast.16), channel_id=1, replica_groups={{0,16,64,80,128,144,192,208},{1,17,65,81,129,145,193,209},{2,18,66,82,1..., dimensions={0} | all-to-all | bytes 131072 | tf_op jit(solution)/shard_map/all_to_all | solution.py:270
  127.2 1.1 shard_map.79
  (39 shorter events, 0.6 us)
Async XLA Ops:
  0.0 1.2 copy-start.4
  3.4 11.3 %collective-permute-start.1 = (bf16[32,7200]{1,0:T(8,128)(2,1)S(1)}, bf16[32,7200]{1,0:T(8,128)(2,1)S(1)}, u32[]{:S(2)}, u32[]{:S(2)}) collective-permute-start(bf16[32,7200]{1,0:T(8,128)(2,1)S(1)} %get-tuple-element.33), channel_id=1, source_target_pairs={{0,16},{16,0},{32,48},{48,32},{64,80},{80,64},{96,112},{112,96},{1... | collective-permute-start | bytes 1382408 | tf_op jit(solution)/shard_map/sib/ppermute | solution.py:37
  6.7 12.3 %collective-permute-start = (bf16[32,7200]{1,0:T(8,128)(2,1)S(1)}, bf16[32,7200]{1,0:T(8,128)(2,1)S(1)}, u32[]{:S(2)}, u32[]{:S(2)}) collective-permute-start(bf16[32,7200]{1,0:T(8,128)(2,1)S(1)} %get-tuple-element.31.refs_0_), channel_id=1, source_target_pairs={{0,192},{16,208},{32,224},{48,240},{64,0},{80,16},{96,32},{112,48}... | collective-permute-start | bytes 1382408 | tf_op jit(solution)/shard_map/r0/ppermute | solution.py:37
  7.7 13.9 %collective-permute-start.2 = (bf16[32,7200]{1,0:T(8,128)(2,1)S(1)}, bf16[32,7200]{1,0:T(8,128)(2,1)S(1)}, u32[]{:S(2)}, u32[]{:S(2)}) collective-permute-start(bf16[32,7200]{1,0:T(8,128)(2,1)S(1)} %get-tuple-element.31.refs_0_), channel_id=1, source_target_pairs={{0,64},{16,80},{32,96},{48,112},{64,128},{80,144},{96,160},{112,17... | collective-permute-start | bytes 1382408 | tf_op jit(solution)/shard_map/l0/ppermute | solution.py:37
  8.2 29.6 %collective-permute-start.7 = (bf16[32,7200]{1,0:T(8,128)(2,1)S(1)}, bf16[32,7200]{1,0:T(8,128)(2,1)S(1)}, u32[]{:S(2)}, u32[]{:S(2)}) collective-permute-start(bf16[32,7200]{1,0:T(8,128)(2,1)S(1)} %get-tuple-element.31.refs_0_), channel_id=1, source_target_pairs={{0,32},{16,48},{32,0},{48,16},{64,96},{80,112},{96,64},{112,80},{1... | collective-permute-start | bytes 1382408 | tf_op jit(solution)/shard_map/z0/ppermute | solution.py:37
  14.7 3.1 %copy-start.5 = (bf16[16,900,256]{2,0,1:T(8,128)(2,1)S(1)}, bf16[16,900,256]{2,0,1:T(8,128)(2,1)}, u32[]{:S(2)}) copy-start(bf16[16,900,256]{2,0,1:T(8,128)(2,1)} %param.7) | copy-start | bytes 22118404
  18.0 57.6 %collective-permute-start.8 = (bf16[900,8,256]{2,1,0:T(8,128)(2,1)S(1)}, bf16[900,8,256]{2,1,0:T(8,128)(2,1)S(1)}, u32[]{:S(2)}, u32[]{:S(2)}) collective-permute-start(bf16[900,8,256]{2,1,0:T(8,128)(2,1)S(1)} %dynamic-slice_bitcast_fusion.1), channel_id=1, source_target_pairs={{0,16},{16,0},{32,48},{48,32},{64,80},{80,64},{96,112},{112,96},{1... | collective-permute-start | bytes 11059208 | tf_op jit(solution)/shard_map/ints/ppermute | solution.py:37
  18.7 13.9 %collective-permute-start.5 = (bf16[32,7200]{1,0:T(8,128)(2,1)S(1)}, bf16[32,7200]{1,0:T(8,128)(2,1)S(1)}, u32[]{:S(2)}, u32[]{:S(2)}) collective-permute-start(bf16[32,7200]{1,0:T(8,128)(2,1)S(1)} %collective-permute-done.1.refs_4_), channel_id=1, source_target_pairs={{0,64},{16,80},{32,96},{48,112},{64,128},{80,144},{96,160},{112,17... | collective-permute-start | bytes 1382408 | tf_op jit(solution)/shard_map/l1/ppermute | solution.py:37
  19.1 18.7 %collective-permute-start.4 = (bf16[32,7200]{1,0:T(8,128)(2,1)S(1)}, bf16[32,7200]{1,0:T(8,128)(2,1)S(1)}, u32[]{:S(2)}, u32[]{:S(2)}) collective-permute-start(bf16[32,7200]{1,0:T(8,128)(2,1)S(1)} %collective-permute-done.1.refs_4_), channel_id=1, source_target_pairs={{0,192},{16,208},{32,224},{48,240},{64,0},{80,16},{96,32},{112,48}... | collective-permute-start | bytes 1382408 | tf_op jit(solution)/shard_map/r1/ppermute | solution.py:37
  21.7 19.7 %collective-permute-start.3 = (bf16[32,7200]{1,0:T(8,128)(2,1)S(1)}, bf16[32,7200]{1,0:T(8,128)(2,1)S(1)}, u32[]{:S(2)}, u32[]{:S(2)}) collective-permute-start(bf16[32,7200]{1,0:T(8,128)(2,1)S(1)} %collective-permute-done.refs_1_), channel_id=1, source_target_pairs={{0,192},{16,208},{32,224},{48,240},{64,0},{80,16},{96,32},{112,48}... | collective-permute-start | bytes 1382408 | tf_op jit(solution)/shard_map/f0/ppermute | solution.py:37
  32.6 20.5 %collective-permute-start.11 = (bf16[32,7200]{1,0:T(8,128)(2,1)S(1)}, bf16[32,7200]{1,0:T(8,128)(2,1)S(1)}, u32[]{:S(2)}, u32[]{:S(2)}) collective-permute-start(bf16[32,7200]{1,0:T(8,128)(2,1)S(1)} %collective-permute-done.1.refs_4_), channel_id=1, source_target_pairs={{0,32},{16,48},{32,0},{48,16},{64,96},{80,112},{96,64},{112,80},{1... | collective-permute-start | bytes 1382408 | tf_op jit(solution)/shard_map/z1/ppermute | solution.py:37
  37.8 15.4 %collective-permute-start.6 = (bf16[32,7200]{1,0:T(8,128)(2,1)S(1)}, bf16[32,7200]{1,0:T(8,128)(2,1)S(1)}, u32[]{:S(2)}, u32[]{:S(2)}) collective-permute-start(bf16[32,7200]{1,0:T(8,128)(2,1)S(1)} %collective-permute-done.5.refs_7_), channel_id=1, source_target_pairs={{0,64},{16,80},{32,96},{48,112},{64,128},{80,144},{96,160},{112,17... | collective-permute-start | bytes 1382408 | tf_op jit(solution)/shard_map/f1/ppermute | solution.py:37
  37.8 24.8 %collective-permute-start.10 = (bf16[32,7200]{1,0:T(8,128)(2,1)S(1)}, bf16[32,7200]{1,0:T(8,128)(2,1)S(1)}, u32[]{:S(2)}, u32[]{:S(2)}) collective-permute-start(bf16[32,7200]{1,0:T(8,128)(2,1)S(1)} %collective-permute-done.7.refs_0_), channel_id=1, source_target_pairs={{0,64},{16,80},{32,96},{48,112},{64,128},{80,144},{96,160},{112,17... | collective-permute-start | bytes 1382408 | tf_op jit(solution)/shard_map/zl0/ppermute | solution.py:37
  41.4 21.2 %collective-permute-start.9 = (bf16[32,7200]{1,0:T(8,128)(2,1)S(1)}, bf16[32,7200]{1,0:T(8,128)(2,1)S(1)}, u32[]{:S(2)}, u32[]{:S(2)}) collective-permute-start(bf16[32,7200]{1,0:T(8,128)(2,1)S(1)} %collective-permute-done.7.refs_0_), channel_id=1, source_target_pairs={{0,192},{16,208},{32,224},{48,240},{64,0},{80,16},{96,32},{112,48}... | collective-permute-start | bytes 1382408 | tf_op jit(solution)/shard_map/zr0/ppermute | solution.py:37
  53.2 19.0 %collective-permute-start.13 = (bf16[32,7200]{1,0:T(8,128)(2,1)S(1)}, bf16[32,7200]{1,0:T(8,128)(2,1)S(1)}, u32[]{:S(2)}, u32[]{:S(2)}) collective-permute-start(bf16[32,7200]{1,0:T(8,128)(2,1)S(1)} %collective-permute-done.11.refs_4_), channel_id=1, source_target_pairs={{0,192},{16,208},{32,224},{48,240},{64,0},{80,16},{96,32},{112,48}... | collective-permute-start | bytes 1382408 | tf_op jit(solution)/shard_map/zr1/ppermute | solution.py:37
  62.6 22.7 %collective-permute-start.15 = (bf16[32,7200]{1,0:T(8,128)(2,1)S(1)}, bf16[32,7200]{1,0:T(8,128)(2,1)S(1)}, u32[]{:S(2)}, u32[]{:S(2)}) collective-permute-start(bf16[32,7200]{1,0:T(8,128)(2,1)S(1)} %collective-permute-done.11.refs_4_), channel_id=1, source_target_pairs={{0,64},{16,80},{32,96},{48,112},{64,128},{80,144},{96,160},{112,17... | collective-permute-start | bytes 1382408 | tf_op jit(solution)/shard_map/zl1/ppermute | solution.py:37
  62.6 22.6 %collective-permute-start.12 = (bf16[32,7200]{1,0:T(8,128)(2,1)S(1)}, bf16[32,7200]{1,0:T(8,128)(2,1)S(1)}, u32[]{:S(2)}, u32[]{:S(2)}) collective-permute-start(bf16[32,7200]{1,0:T(8,128)(2,1)S(1)} %collective-permute-done.10.refs_3_), channel_id=1, source_target_pairs={{0,64},{16,80},{32,96},{48,112},{64,128},{80,144},{96,160},{112,17... | collective-permute-start | bytes 1382408 | tf_op jit(solution)/shard_map/zf0/ppermute | solution.py:37
  72.2 13.1 %collective-permute-start.14 = (bf16[32,7200]{1,0:T(8,128)(2,1)S(1)}, bf16[32,7200]{1,0:T(8,128)(2,1)S(1)}, u32[]{:S(2)}, u32[]{:S(2)}) collective-permute-start(bf16[32,7200]{1,0:T(8,128)(2,1)S(1)} %collective-permute-done.13.refs_5_), channel_id=1, source_target_pairs={{0,192},{16,208},{32,224},{48,240},{64,0},{80,16},{96,32},{112,48}... | collective-permute-start | bytes 1382408 | tf_op jit(solution)/shard_map/zf1/ppermute | solution.py:37
  76.8 2.9 %collective-permute-start.16 = (f32[256,256]{1,0:T(8,128)S(1)}, f32[256,256]{1,0:T(8,128)S(1)}, u32[]{:S(2)}, u32[]{:S(2)}) collective-permute-start(f32[256,256]{1,0:T(8,128)S(1)} %shard_map.70), channel_id=1, source_target_pairs={{0,16},{16,0},{32,48},{48,32},{64,80},{80,64},{96,112},{112,96},{1... | collective-permute-start | bytes 786440 | tf_op jit(solution)/shard_map/t0/ppermute | solution.py:37
  86.5 3.0 %collective-permute-start.17 = (f32[256,256]{1,0:T(8,128)S(1)}, f32[256,256]{1,0:T(8,128)S(1)}, u32[]{:S(2)}, u32[]{:S(2)}) collective-permute-start(f32[256,256]{1,0:T(8,128)S(1)} %shard_map.75), channel_id=1, source_target_pairs={{0,16},{16,0},{32,48},{48,32},{64,80},{80,64},{96,112},{112,96},{1... | collective-permute-start | bytes 786440 | tf_op jit(solution)/shard_map/t1/ppermute | solution.py:37
  89.4 37.7 %copy-start = (bf16[32,256]{1,0:T(8,128)(2,1)S(1)}, bf16[32,256]{1,0:T(8,128)(2,1)}, u32[]{:S(2)}) copy-start(bf16[32,256]{1,0:T(8,128)(2,1)} %other_ref.1) | copy-start | bytes 49156
  89.4 37.7 %copy-start.1 = (s32[32,2]{0,1:T(2,128)S(1)}, s32[32,2]{0,1:T(2,128)}, u32[]{:S(2)}) copy-start(s32[32,2]{0,1:T(2,128)} %param.11) | copy-start | bytes 772
  89.4 37.7 %copy-start.2 = (f32[60]{0:T(128)S(1)}, f32[60]{0:T(128)}, u32[]{:S(2)}) copy-start(f32[60]{0:T(128)} %param.9) | copy-start | bytes 724
  89.4 37.7 %copy-start.3 = (f32[64]{0:T(128)S(1)}, f32[64]{0:T(128)}, u32[]{:S(2)}) copy-start(f32[64]{0:T(128)} %param.10) | copy-start | bytes 772

commit v3 on v2

--- a/solution.py
+++ b/solution.py
@@ -274,36 +274,35 @@
 
 def local(lambda_cd, integrals, other_terms, hole_energy, virtual_energy, pair_orbitals):
     core = lax.axis_index("bulk") % 2
+    shift = bulk_shift
     own, other, g = pack(lambda_cd)
-    shift = bulk_shift
     z0 = shift("z0", own, dh=1)
-    sib = shift("sib", other, dc=1)
     r0 = shift("r0", own, dy=-1)
     l0 = shift("l0", own, dy=1)
+    sib = shift("sib", other, dc=1)
     g = stage(g, sib, cost=COSTS[0])
     l1 = shift("l1", after(sib, g), dy=1)
     r1 = shift("r1", after(sib, g), dy=-1)
+    z1 = shift("z1", after(sib, g), dh=1)
+    g = stage(g, r0, l0, cost=COSTS[2])
+    f0 = shift("f0", after(r0, g), dy=-1)
     ints = jnp.transpose(after(integrals, g), (1, 0, 2))
     ints_other = lax.dynamic_slice_in_dim(ints, (1 - core) * C_HALF, C_HALF, axis=1)
     ints_sib = shift("ints", ints_other, dc=1).reshape(K_ALL, COLS)
-    g = stage(g, ints_other, cost=COSTS[1])
-    z1 = shift("z1", after(sib, g), dh=1)
-    g = stage(g, r0, l0, cost=COSTS[2])
-    f0 = shift("f0", after(r0, g), dy=-1)
     g = stage(g, r1, l1, cost=COSTS[3])
     f1 = shift("f1", after(l1, g), dy=1)
     g = stage(g, z0, cost=COSTS[4])
     zr0 = shift("zr0", after(z0, g), dy=-1)
     zl0 = shift("zl0", after(z0, g), dy=1)
+    g = stage(g, z1, f0, f1, cost=COSTS[5])
+    zr1 = shift("zr1", after(z1, g), dy=-1)
+    zl1 = shift("zl1", after(z1, g), dy=1)
+    g = stage(g, zr0, zl0, cost=COSTS[6])
+    zf0 = shift("zf0", after(zl0, g), dy=1)
     ints = jnp.transpose(after(integrals, g), (1, 0, 2))
     ints_own = lax.dynamic_slice_in_dim(ints, core * C_HALF, C_HALF, axis=1)
     ints_own = ints_own.reshape(K_ALL, COLS)
-    g = stage(g, z1, f0, f1, cost=COSTS[5])
-    zr1 = shift("zr1", after(z1, g), dy=-1)
-    zl1 = shift("zl1", after(z1, g), dy=1)
-    g = stage(g, zr0, zl0, ints_own, cost=COSTS[6])
-    zf0 = shift("zf0", after(zl0, g), dy=1)
-    g = stage(g, zr1, cost=COSTS[7])
+    g = stage(g, zr1, ints_own, cost=COSTS[7])
     zf1 = shift("zf1", after(zr1, g), dy=-1)
 
     near = {(0, 0, 0): own, (0, 0, 1): r0, (0, 0, 2): f0, (0, 0, 3): l0}

time: 129 us -> 126 us (0.977)
  blocking collectives: 37.2 us -> 46.3 us
  waiting for transfers between devices: 36.1 us -> 31 us
  starting transfers between devices: 41.4 us -> 38.1 us
  local copies, waits for them, and re-layouts: 4.85 us -> 1.76 us
    all_to_all x3, blocking collectives: 37.2 us -> 46.3 us  [exchange(): lax.all_to_all(value, ('bulk', 'occ'), 0, 0, axis_index_groups=group(kind...]
    ppermute x18, waiting for transfers between devices: 36.1 us -> 31 us  [bulk_shift(): return lax.ppermute(value, 'bulk', pairs)]
    ppermute x18, starting transfers between devices: 41.4 us -> 38.1 us  [bulk_shift(): return lax.ppermute(value, 'bulk', pairs)]
    unnamed x12 -> x14, local copies, waits for them, and re-layouts: 4.34 us -> 1.26 us
where the time goes in v3:
time: 126 us
  blocking collectives  46.3 us (37%)
  starting transfers between devices  38.1 us (30%)
  waiting for transfers between devices  31 us (25%)
  Pallas kernels  8.41 us (7%)
  local copies, waits for them, and re-layouts  1.76 us (1%)
    all_to_all x3, blocking collectives, exchange(): lax.all_to_all(value, ('bulk', 'occ'), 0, 0, axis_index_groups=group(kind...  46.3 us
    ppermute x18, starting transfers between devices, bulk_shift(): return lax.ppermute(value, 'bulk', pairs)  38.1 us
    ppermute x18, waiting for transfers between devices, bulk_shift(): return lax.ppermute(value, 'bulk', pairs)  31 us
    pallas_call x4, Pallas kernels, ladder(): pl.pallas_call(ladder_kernel, out_shape=jax.ShapeDtypeStruct((m, COLS), j...  4.76 us
  transfers between devices with their start and end apart: 18, of which 5 were waited for; matrix products, arithmetic and copies ran while one was open for 0% of the time, Pallas kernels for 3%

profile of v3, /device:TPU:1, one launch (start us, length us, event | category | flops | bytes accessed | tf_op | source)
XLA Modules:
  0.0 125.7 jit_solution(14717616644337892428)
XLA Ops:
  0.0 1.2 copy-done.4
  1.2 2.2 %shard_map.64 = (bf16[32,7200]{1,0:T(8,128)(2,1)S(1)}, bf16[32,7200]{1,0:T(8,128)(2,1)S(1)}, f32[8,128]{1,0:T(8,128)S(1)}) custom-call(bf16[32,16,900]{2,1,0:T(8,128)(2,1)S(1)} %copy-done.4), custom_call_target="tpu_custom_call" | custom-call | flops 471859200 | bytes 2097152 | tf_op jit(solution)/shard_map/pallas_call | solution.py:96
  3.4 3.3 %collective-permute-start.1 = (bf16[32,7200]{1,0:T(8,128)(2,1)S(1)}, bf16[32,7200]{1,0:T(8,128)(2,1)S(1)}, u32[]{:S(2)}, u32[]{:S(2)}) collective-permute-start(bf16[32,7200]{1,0:T(8,128)(2,1)S(1)} %get-tuple-element.31), channel_id=1, source_target_pairs={{0,16},{16,0},{32,48},{48,32},{64,80},{80,64},{96,112},{112,96},{1... | collective-permute-start | bytes 1382408 | tf_op jit(solution)/shard_map/sib/ppermute | solution.py:37
  6.7 1.0 collective-permute-start
  7.7 0.5 collective-permute-start.2
  8.2 6.4 %collective-permute-start.7 = (bf16[32,7200]{1,0:T(8,128)(2,1)S(1)}, bf16[32,7200]{1,0:T(8,128)(2,1)S(1)}, u32[]{:S(2)}, u32[]{:S(2)}) collective-permute-start(bf16[32,7200]{1,0:T(8,128)(2,1)S(1)} %get-tuple-element.29.refs_0_), channel_id=1, source_target_pairs={{0,32},{16,48},{32,0},{48,16},{64,96},{80,112},{96,64},{112,80},{1... | collective-permute-start | bytes 1382408 | tf_op jit(solution)/shard_map/z0/ppermute | solution.py:37
  14.7 0.1 collective-permute-start.5
  14.8 2.7 %collective-permute-start.4 = (bf16[32,7200]{1,0:T(8,128)(2,1)S(1)}, bf16[32,7200]{1,0:T(8,128)(2,1)S(1)}, u32[]{:S(2)}, u32[]{:S(2)}) collective-permute-start(bf16[32,7200]{1,0:T(8,128)(2,1)S(1)} %collective-permute-done.1.refs_4_), channel_id=1, source_target_pairs={{0,192},{16,208},{32,224},{48,240},{64,0},{80,16},{96,32},{112,48}... | collective-permute-start | bytes 1382408 | tf_op jit(solution)/shard_map/r1/ppermute | solution.py:37
  17.5 1.5 %collective-permute-done.refs_1_ = bf16[32,7200]{1,0:T(8,128)(2,1)S(1)} collective-permute-done((bf16[32,7200]{1,0:T(8,128)(2,1)S(1)}, bf16[32,7200]{1,0:T(8,128)(2,1)S(1)}, u32[]{:S(2)}, u32[]{:S(2)}) %collective-permute-start) | collective-permute-done | bytes 460832 | tf_op jit(solution)/shard_map/r0/ppermute | solution.py:37
  19.0 5.7 %collective-permute-start.8 = (bf16[32,7200]{1,0:T(8,128)(2,1)S(1)}, bf16[32,7200]{1,0:T(8,128)(2,1)S(1)}, u32[]{:S(2)}, u32[]{:S(2)}) collective-permute-start(bf16[32,7200]{1,0:T(8,128)(2,1)S(1)} %collective-permute-done.1.refs_4_), channel_id=1, source_target_pairs={{0,32},{16,48},{32,0},{48,16},{64,96},{80,112},{96,64},{112,80},{1... | collective-permute-start | bytes 1382408 | tf_op jit(solution)/shard_map/z1/ppermute | solution.py:37
  24.7 0.2 dynamic-slice_bitcast_fusion
  25.0 1.7 %collective-permute-start.11 = (bf16[900,8,256]{2,1,0:T(8,128)(2,1)S(1)}, bf16[900,8,256]{2,1,0:T(8,128)(2,1)S(1)}, u32[]{:S(2)}, u32[]{:S(2)}) collective-permute-start(bf16[900,8,256]{2,1,0:T(8,128)(2,1)S(1)} %dynamic-slice_bitcast_fusion), channel_id=1, source_target_pairs={{0,16},{16,0},{32,48},{48,32},{64,80},{80,64},{96,112},{112,96},{1... | collective-permute-start | bytes 11059208 | tf_op jit(solution)/shard_map/ints/ppermute | solution.py:37
  26.7 4.2 %collective-permute-done.5.refs_7_ = bf16[32,7200]{1,0:T(8,128)(2,1)S(1)} collective-permute-done((bf16[32,7200]{1,0:T(8,128)(2,1)S(1)}, bf16[32,7200]{1,0:T(8,128)(2,1)S(1)}, u32[]{:S(2)}, u32[]{:S(2)}) %collective-permute-start.5) | collective-permute-done | bytes 460832 | tf_op jit(solution)/shard_map/l1/ppermute | solution.py:37
  30.9 1.5 %collective-permute-start.6 = (bf16[32,7200]{1,0:T(8,128)(2,1)S(1)}, bf16[32,7200]{1,0:T(8,128)(2,1)S(1)}, u32[]{:S(2)}, u32[]{:S(2)}) collective-permute-start(bf16[32,7200]{1,0:T(8,128)(2,1)S(1)} %collective-permute-done.5.refs_7_), channel_id=1, source_target_pairs={{0,64},{16,80},{32,96},{48,112},{64,128},{80,144},{96,160},{112,17... | collective-permute-start | bytes 1382408 | tf_op jit(solution)/shard_map/f1/ppermute | solution.py:37
  32.5 9.4 %collective-permute-done.3.refs_2_ = bf16[32,7200]{1,0:T(8,128)(2,1)S(1)} collective-permute-done((bf16[32,7200]{1,0:T(8,128)(2,1)S(1)}, bf16[32,7200]{1,0:T(8,128)(2,1)S(1)}, u32[]{:S(2)}, u32[]{:S(2)}) %collective-permute-start.3) | collective-permute-done | bytes 460832 | tf_op jit(solution)/shard_map/f0/ppermute | solution.py:37
  41.9 1.5 %collective-permute-start.9 = (bf16[32,7200]{1,0:T(8,128)(2,1)S(1)}, bf16[32,7200]{1,0:T(8,128)(2,1)S(1)}, u32[]{:S(2)}, u32[]{:S(2)}) collective-permute-start(bf16[32,7200]{1,0:T(8,128)(2,1)S(1)} %collective-permute-done.7.refs_0_), channel_id=1, source_target_pairs={{0,192},{16,208},{32,224},{48,240},{64,0},{80,16},{96,32},{112,48}... | collective-permute-start | bytes 1382408 | tf_op jit(solution)/shard_map/zr0/ppermute | solution.py:37
  43.5 1.4 %collective-permute-start.15 = (bf16[32,7200]{1,0:T(8,128)(2,1)S(1)}, bf16[32,7200]{1,0:T(8,128)(2,1)S(1)}, u32[]{:S(2)}, u32[]{:S(2)}) collective-permute-start(bf16[32,7200]{1,0:T(8,128)(2,1)S(1)} %collective-permute-done.8.refs_4_), channel_id=1, source_target_pairs={{0,64},{16,80},{32,96},{48,112},{64,128},{80,144},{96,160},{112,17... | collective-permute-start | bytes 1382408 | tf_op jit(solution)/shard_map/zl1/ppermute | solution.py:37
  44.9 8.3 %collective-permute-done.10.refs_3_ = bf16[32,7200]{1,0:T(8,128)(2,1)S(1)} collective-permute-done((bf16[32,7200]{1,0:T(8,128)(2,1)S(1)}, bf16[32,7200]{1,0:T(8,128)(2,1)S(1)}, u32[]{:S(2)}, u32[]{:S(2)}) %collective-permute-start.10) | collective-permute-done | bytes 460832 | tf_op jit(solution)/shard_map/zl0/ppermute | solution.py:37
  53.2 0.2 dynamic-slice_bitcast_fusion.1.refs_8_
  53.4 7.5 %collective-permute-done.13.refs_5_ = bf16[32,7200]{1,0:T(8,128)(2,1)S(1)} collective-permute-done((bf16[32,7200]{1,0:T(8,128)(2,1)S(1)}, bf16[32,7200]{1,0:T(8,128)(2,1)S(1)}, u32[]{:S(2)}, u32[]{:S(2)}) %collective-permute-start.13) | collective-permute-done | bytes 460832 | tf_op jit(solution)/shard_map/zr1/ppermute | solution.py:37
  60.9 1.6 %collective-permute-start.14 = (bf16[32,7200]{1,0:T(8,128)(2,1)S(1)}, bf16[32,7200]{1,0:T(8,128)(2,1)S(1)}, u32[]{:S(2)}, u32[]{:S(2)}) collective-permute-start(bf16[32,7200]{1,0:T(8,128)(2,1)S(1)} %collective-permute-done.13.refs_5_), channel_id=1, source_target_pairs={{0,192},{16,208},{32,224},{48,240},{64,0},{80,16},{96,32},{112,48}... | collective-permute-start | bytes 1382408 | tf_op jit(solution)/shard_map/zf1/ppermute | solution.py:37
  62.5 1.2 shard_map.71
  63.7 6.5 %collective-permute-start.16 = (f32[256,256]{1,0:T(8,128)S(1)}, f32[256,256]{1,0:T(8,128)S(1)}, u32[]{:S(2)}, u32[]{:S(2)}) collective-permute-start(f32[256,256]{1,0:T(8,128)S(1)} %shard_map.71), channel_id=1, source_target_pairs={{0,16},{16,0},{32,48},{48,32},{64,80},{80,64},{96,112},{112,96},{1... | collective-permute-start | bytes 786440 | tf_op jit(solution)/shard_map/t0/ppermute | solution.py:37
  70.2 1.2 shard_map.72.refs_0_
  71.4 1.2 shard_map.74
  72.6 4.0 %collective-permute-start.17 = (f32[256,256]{1,0:T(8,128)S(1)}, f32[256,256]{1,0:T(8,128)S(1)}, u32[]{:S(2)}, u32[]{:S(2)}) collective-permute-start(f32[256,256]{1,0:T(8,128)S(1)} %shard_map.74), channel_id=1, source_target_pairs={{0,16},{16,0},{32,48},{48,32},{64,80},{80,64},{96,112},{112,96},{1... | collective-permute-start | bytes 786440 | tf_op jit(solution)/shard_map/t1/ppermute | solution.py:37
  76.6 1.2 shard_map.75.refs_1_
  77.9 12.8 %all_to_all.15 = f32[4,4,32,256]{3,2,1,0:T(8,128)S(1)} all-to-all(f32[4,4,32,256]{3,2,1,0:T(8,128)S(1)} %shard_map.76), channel_id=1, replica_groups={{0,4,8,12},{1,5,9,13},{2,6,10,14},{3,7,11,15},{16,20,24,28},{17,21,25,2..., dimensions={0} | all-to-all | bytes 1048576 | tf_op jit(solution)/shard_map/all_to_all | solution.py:270
  90.8 22.2 %all_to_all.16.t_ref = f32[8,32,256]{2,1,0:T(8,128)S(1)} all-to-all(f32[8,32,256]{2,1,0:T(8,128)S(1)} %bitcast.22), channel_id=1, replica_groups={{0,1,2,3,32,33,34,35},{4,5,6,7,36,37,38,39},{8,9,10,11,40,41,42,43},{12..., dimensions={0} | all-to-all | bytes 524288 | tf_op jit(solution)/shard_map/all_to_all | solution.py:270
  113.1 0.3 shard_map.77
  113.4 11.2 %all_to_all.17 = f32[8,16,128]{2,1,0:T(8,128)S(1)} all-to-all(f32[8,16,128]{2,1,0:T(8,128)S(1)} %bitcast.16), channel_id=1, replica_groups={{0,16,64,80,128,144,192,208},{1,17,65,81,129,145,193,209},{2,18,66,82,1..., dimensions={0} | all-to-all | bytes 131072 | tf_op jit(solution)/shard_map/all_to_all | solution.py:270
  124.6 1.1 shard_map.78
  (41 shorter events, 0.4 us)
Async XLA Ops:
  0.0 1.2 copy-start.4
  3.4 11.3 %collective-permute-start.1 = (bf16[32,7200]{1,0:T(8,128)(2,1)S(1)}, bf16[32,7200]{1,0:T(8,128)(2,1)S(1)}, u32[]{:S(2)}, u32[]{:S(2)}) collective-permute-start(bf16[32,7200]{1,0:T(8,128)(2,1)S(1)} %get-tuple-element.31), channel_id=1, source_target_pairs={{0,16},{16,0},{32,48},{48,32},{64,80},{80,64},{96,112},{112,96},{1... | collective-permute-start | bytes 1382408 | tf_op jit(solution)/shard_map/sib/ppermute | solution.py:37
  6.7 12.3 %collective-permute-start = (bf16[32,7200]{1,0:T(8,128)(2,1)S(1)}, bf16[32,7200]{1,0:T(8,128)(2,1)S(1)}, u32[]{:S(2)}, u32[]{:S(2)}) collective-permute-start(bf16[32,7200]{1,0:T(8,128)(2,1)S(1)} %get-tuple-element.29.refs_0_), channel_id=1, source_target_pairs={{0,192},{16,208},{32,224},{48,240},{64,0},{80,16},{96,32},{112,48}... | collective-permute-start | bytes 1382408 | tf_op jit(solution)/shard_map/r0/ppermute | solution.py:37
  7.7 17.0 %collective-permute-start.2 = (bf16[32,7200]{1,0:T(8,128)(2,1)S(1)}, bf16[32,7200]{1,0:T(8,128)(2,1)S(1)}, u32[]{:S(2)}, u32[]{:S(2)}) collective-permute-start(bf16[32,7200]{1,0:T(8,128)(2,1)S(1)} %get-tuple-element.29.refs_0_), channel_id=1, source_target_pairs={{0,64},{16,80},{32,96},{48,112},{64,128},{80,144},{96,160},{112,17... | collective-permute-start | bytes 1382408 | tf_op jit(solution)/shard_map/l0/ppermute | solution.py:37
  8.2 24.1 %collective-permute-start.7 = (bf16[32,7200]{1,0:T(8,128)(2,1)S(1)}, bf16[32,7200]{1,0:T(8,128)(2,1)S(1)}, u32[]{:S(2)}, u32[]{:S(2)}) collective-permute-start(bf16[32,7200]{1,0:T(8,128)(2,1)S(1)} %get-tuple-element.29.refs_0_), channel_id=1, source_target_pairs={{0,32},{16,48},{32,0},{48,16},{64,96},{80,112},{96,64},{112,80},{1... | collective-permute-start | bytes 1382408 | tf_op jit(solution)/shard_map/z0/ppermute | solution.py:37
  14.7 10.0 %slice-start = ((s8[7372800]{0:T(1024)(128)(4,1)}), s8[4194304]{0:T(1024)(128)(4,1)S(1)}, s32[]{:S(2)}) async-start(s8[7372800]{0:T(1024)(128)(4,1)} %bitcast.20), calls=%async_computation.3 | async-start | bytes 8388608
  14.7 10.0 %slice-start.1 = ((s8[7372800]{0:T(1024)(128)(4,1)}), s8[3178496]{0:T(1024)(128)(4,1)S(1)}, s32[]{:S(2)}) async-start(s8[7372800]{0:T(1024)(128)(4,1)} %bitcast.20), calls=%async_computation.4 | async-start | bytes 6356992
  14.7 16.2 %collective-permute-start.5 = (bf16[32,7200]{1,0:T(8,128)(2,1)S(1)}, bf16[32,7200]{1,0:T(8,128)(2,1)S(1)}, u32[]{:S(2)}, u32[]{:S(2)}) collective-permute-start(bf16[32,7200]{1,0:T(8,128)(2,1)S(1)} %collective-permute-done.1.refs_4_), channel_id=1, source_target_pairs={{0,64},{16,80},{32,96},{48,112},{64,128},{80,144},{96,160},{112,17... | collective-permute-start | bytes 1382408 | tf_op jit(solution)/shard_map/l1/ppermute | solution.py:37
  14.8 16.1 %collective-permute-start.4 = (bf16[32,7200]{1,0:T(8,128)(2,1)S(1)}, bf16[32,7200]{1,0:T(8,128)(2,1)S(1)}, u32[]{:S(2)}, u32[]{:S(2)}) collective-permute-start(bf16[32,7200]{1,0:T(8,128)(2,1)S(1)} %collective-permute-done.1.refs_4_), channel_id=1, source_target_pairs={{0,192},{16,208},{32,224},{48,240},{64,0},{80,16},{96,32},{112,48}... | collective-permute-start | bytes 1382408 | tf_op jit(solution)/shard_map/r1/ppermute | solution.py:37
  19.0 24.4 %collective-permute-start.8 = (bf16[32,7200]{1,0:T(8,128)(2,1)S(1)}, bf16[32,7200]{1,0:T(8,128)(2,1)S(1)}, u32[]{:S(2)}, u32[]{:S(2)}) collective-permute-start(bf16[32,7200]{1,0:T(8,128)(2,1)S(1)} %collective-permute-done.1.refs_4_), channel_id=1, source_target_pairs={{0,32},{16,48},{32,0},{48,16},{64,96},{80,112},{96,64},{112,80},{1... | collective-permute-start | bytes 1382408 | tf_op jit(solution)/shard_map/z1/ppermute | solution.py:37
  25.0 37.5 %collective-permute-start.11 = (bf16[900,8,256]{2,1,0:T(8,128)(2,1)S(1)}, bf16[900,8,256]{2,1,0:T(8,128)(2,1)S(1)}, u32[]{:S(2)}, u32[]{:S(2)}) collective-permute-start(bf16[900,8,256]{2,1,0:T(8,128)(2,1)S(1)} %dynamic-slice_bitcast_fusion), channel_id=1, source_target_pairs={{0,16},{16,0},{32,48},{48,32},{64,80},{80,64},{96,112},{112,96},{1... | collective-permute-start | bytes 11059208 | tf_op jit(solution)/shard_map/ints/ppermute | solution.py:37
  30.9 11.0 %collective-permute-start.3 = (bf16[32,7200]{1,0:T(8,128)(2,1)S(1)}, bf16[32,7200]{1,0:T(8,128)(2,1)S(1)}, u32[]{:S(2)}, u32[]{:S(2)}) collective-permute-start(bf16[32,7200]{1,0:T(8,128)(2,1)S(1)} %collective-permute-done.refs_1_), channel_id=1, source_target_pairs={{0,192},{16,208},{32,224},{48,240},{64,0},{80,16},{96,32},{112,48}... | collective-permute-start | bytes 1382408 | tf_op jit(solution)/shard_map/f0/ppermute | solution.py:37
  30.9 12.5 %collective-permute-start.6 = (bf16[32,7200]{1,0:T(8,128)(2,1)S(1)}, bf16[32,7200]{1,0:T(8,128)(2,1)S(1)}, u32[]{:S(2)}, u32[]{:S(2)}) collective-permute-start(bf16[32,7200]{1,0:T(8,128)(2,1)S(1)} %collective-permute-done.5.refs_7_), channel_id=1, source_target_pairs={{0,64},{16,80},{32,96},{48,112},{64,128},{80,144},{96,160},{112,17... | collective-permute-start | bytes 1382408 | tf_op jit(solution)/shard_map/f1/ppermute | solution.py:37
  32.4 20.8 %collective-permute-start.10 = (bf16[32,7200]{1,0:T(8,128)(2,1)S(1)}, bf16[32,7200]{1,0:T(8,128)(2,1)S(1)}, u32[]{:S(2)}, u32[]{:S(2)}) collective-permute-start(bf16[32,7200]{1,0:T(8,128)(2,1)S(1)} %collective-permute-done.7.refs_0_), channel_id=1, source_target_pairs={{0,64},{16,80},{32,96},{48,112},{64,128},{80,144},{96,160},{112,17... | collective-permute-start | bytes 1382408 | tf_op jit(solution)/shard_map/zl0/ppermute | solution.py:37
  41.9 11.3 %collective-permute-start.9 = (bf16[32,7200]{1,0:T(8,128)(2,1)S(1)}, bf16[32,7200]{1,0:T(8,128)(2,1)S(1)}, u32[]{:S(2)}, u32[]{:S(2)}) collective-permute-start(bf16[32,7200]{1,0:T(8,128)(2,1)S(1)} %collective-permute-done.7.refs_0_), channel_id=1, source_target_pairs={{0,192},{16,208},{32,224},{48,240},{64,0},{80,16},{96,32},{112,48}... | collective-permute-start | bytes 1382408 | tf_op jit(solution)/shard_map/zr0/ppermute | solution.py:37
  43.4 17.5 %collective-permute-start.13 = (bf16[32,7200]{1,0:T(8,128)(2,1)S(1)}, bf16[32,7200]{1,0:T(8,128)(2,1)S(1)}, u32[]{:S(2)}, u32[]{:S(2)}) collective-permute-start(bf16[32,7200]{1,0:T(8,128)(2,1)S(1)} %collective-permute-done.8.refs_4_), channel_id=1, source_target_pairs={{0,192},{16,208},{32,224},{48,240},{64,0},{80,16},{96,32},{112,48}... | collective-permute-start | bytes 1382408 | tf_op jit(solution)/shard_map/zr1/ppermute | solution.py:37
  43.5 27.9 %collective-permute-start.15 = (bf16[32,7200]{1,0:T(8,128)(2,1)S(1)}, bf16[32,7200]{1,0:T(8,128)(2,1)S(1)}, u32[]{:S(2)}, u32[]{:S(2)}) collective-permute-start(bf16[32,7200]{1,0:T(8,128)(2,1)S(1)} %collective-permute-done.8.refs_4_), channel_id=1, source_target_pairs={{0,64},{16,80},{32,96},{48,112},{64,128},{80,144},{96,160},{112,17... | collective-permute-start | bytes 1382408 | tf_op jit(solution)/shard_map/zl1/ppermute | solution.py:37
  53.2 18.2 %collective-permute-start.12 = (bf16[32,7200]{1,0:T(8,128)(2,1)S(1)}, bf16[32,7200]{1,0:T(8,128)(2,1)S(1)}, u32[]{:S(2)}, u32[]{:S(2)}) collective-permute-start(bf16[32,7200]{1,0:T(8,128)(2,1)S(1)} %collective-permute-done.10.refs_3_), channel_id=1, source_target_pairs={{0,64},{16,80},{32,96},{48,112},{64,128},{80,144},{96,160},{112,17... | collective-permute-start | bytes 1382408 | tf_op jit(solution)/shard_map/zf0/ppermute | solution.py:37
  60.9 10.5 %collective-permute-start.14 = (bf16[32,7200]{1,0:T(8,128)(2,1)S(1)}, bf16[32,7200]{1,0:T(8,128)(2,1)S(1)}, u32[]{:S(2)}, u32[]{:S(2)}) collective-permute-start(bf16[32,7200]{1,0:T(8,128)(2,1)S(1)} %collective-permute-done.13.refs_5_), channel_id=1, source_target_pairs={{0,192},{16,208},{32,224},{48,240},{64,0},{80,16},{96,32},{112,48}... | collective-permute-start | bytes 1382408 | tf_op jit(solution)/shard_map/zf1/ppermute | solution.py:37
  63.7 7.7 %collective-permute-start.16 = (f32[256,256]{1,0:T(8,128)S(1)}, f32[256,256]{1,0:T(8,128)S(1)}, u32[]{:S(2)}, u32[]{:S(2)}) collective-permute-start(f32[256,256]{1,0:T(8,128)S(1)} %shard_map.71), channel_id=1, source_target_pairs={{0,16},{16,0},{32,48},{48,32},{64,80},{80,64},{96,112},{112,96},{1... | collective-permute-start | bytes 786440 | tf_op jit(solution)/shard_map/t0/ppermute | solution.py:37
  72.6 5.2 %collective-permute-start.17 = (f32[256,256]{1,0:T(8,128)S(1)}, f32[256,256]{1,0:T(8,128)S(1)}, u32[]{:S(2)}, u32[]{:S(2)}) collective-permute-start(f32[256,256]{1,0:T(8,128)S(1)} %shard_map.74), channel_id=1, source_target_pairs={{0,16},{16,0},{32,48},{48,32},{64,80},{80,64},{96,112},{112,96},{1... | collective-permute-start | bytes 786440 | tf_op jit(solution)/shard_map/t1/ppermute | solution.py:37
  77.8 46.8 %copy-start = (bf16[32,256]{1,0:T(8,128)(2,1)S(1)}, bf16[32,256]{1,0:T(8,128)(2,1)}, u32[]{:S(2)}) copy-start(bf16[32,256]{1,0:T(8,128)(2,1)} %other_ref.1) | copy-start | bytes 49156
  77.8 46.8 %copy-start.1 = (s32[32,2]{0,1:T(2,128)S(1)}, s32[32,2]{0,1:T(2,128)}, u32[]{:S(2)}) copy-start(s32[32,2]{0,1:T(2,128)} %param.11) | copy-start | bytes 772
  77.8 46.8 %copy-start.2 = (f32[60]{0:T(128)S(1)}, f32[60]{0:T(128)}, u32[]{:S(2)}) copy-start(f32[60]{0:T(128)} %param.9) | copy-start | bytes 724
  77.8 46.8 %copy-start.3 = (f32[64]{0:T(128)S(1)}, f32[64]{0:T(128)}, u32[]{:S(2)}) copy-start(f32[64]{0:T(128)} %param.10) | copy-start | bytes 772

commit v4 on v3

--- a/solution.py
+++ b/solution.py
@@ -45,19 +45,14 @@
     _, _, core = here()
     token_ref[...] = jnp.zeros_like(token_ref)
     n = ROWS * 16
-    row = lax.broadcasted_iota(jnp.int32, (n, n), 0)
-    col = lax.broadcasted_iota(jnp.int32, (n, n), 1)
-    c = ((row // 256 + core) % 2) * C_HALF + (row % 256) // ROWS
-    perm = jnp.where(col == (row % ROWS) * 16 + c, 1.0, 0.0).astype(jnp.bfloat16)
-    lam = lam_ref[...].reshape(n, D)
     full = D // 128 * 128
-    main = jnp.dot(perm, lam[:, :full], preferred_element_type=jnp.float32)
-    main = main.astype(jnp.bfloat16)
-    rest = jnp.dot(perm, lam[:, full:], preferred_element_type=jnp.float32)
-    rest = rest.astype(jnp.bfloat16)
-    source = lax.broadcasted_iota(jnp.int32, (1024, 1024), 0)
-    goal = lax.broadcasted_iota(jnp.int32, (1024, 1024), 1)
-    weave = jnp.where(goal == (source % 128) * C_HALF + source // 128, 1.0, 0.0)
+    lam = jnp.transpose(lam_ref[...].astype(jnp.float32), (1, 0, 2))
+    turned = jnp.concatenate([lam[C_HALF:], lam[:C_HALF]], axis=0)
+    lam = jnp.where(core == 0, lam, turned).astype(jnp.bfloat16).reshape(n, D)
+    main, rest = lam[:, :full], lam[:, full:]
+    col = lax.broadcasted_iota(jnp.int32, (1, 1024), 1)
+    row = lax.broadcasted_iota(jnp.int32, (1024, 1024), 0)
+    weave = jnp.where(row == col % C_HALF * 128 + col // C_HALF, 1.0, 0.0)
     weave = weave.astype(jnp.bfloat16)
     tail = D - full
     source = lax.broadcasted_iota(jnp.int32, (tail, tail * C_HALF), 0)
@@ -211,8 +206,44 @@
     )(t)
 
 
-def final_kernel(t_ref, mine_ref, other_ref, hole_ref, virt_ref, pairs_ref, token_ref, out_ref):
+def denom_kernel(hole_ref, virt_ref, pairs_ref, out_ref):
     y, h, core = here()
+    exact = dict(precision=lax.Precision.HIGHEST, preferred_element_type=jnp.float32)
+    row = lax.broadcasted_iota(jnp.int32, (VW, COLS), 0)
+    col = lax.broadcasted_iota(jnp.int32, (VW, COLS), 1)
+    own_a = ((y * 2 + h) * 2 + core) * 4 + col // VW
+    pick_a = jnp.where(row == own_a, 1.0, 0.0)
+    pick_b = jnp.where(row == col % VW, 1.0, 0.0)
+    virtual = jnp.broadcast_to(virt_ref[...], (8, VW))
+    virt_a = jnp.dot(virtual, pick_a, **exact)[:1]
+    virt_b = jnp.dot(virtual, pick_b, **exact)[:1]
+    count = hole_ref.shape[1]
+    orbital = lax.broadcasted_iota(jnp.int32, (count, ROWS), 0)
+    hole = jnp.broadcast_to(hole_ref[...], (8, count))
+    diagonal = lax.broadcasted_iota(jnp.int32, (ROWS, ROWS), 0) == lax.broadcasted_iota(
+        jnp.int32, (ROWS, ROWS), 1
+    )
+    holes = jnp.zeros((ROWS, 1), jnp.float32)
+    for k in range(2):
+        pick = jnp.where(orbital == pairs_ref[k : k + 1, :], 1.0, 0.0)
+        energy = jnp.dot(hole, pick, **exact)[:1]
+        holes += jnp.sum(jnp.where(diagonal, energy, 0.0), axis=1, keepdims=True)
+    out_ref[...] = holes + virt_a + virt_b
+
+
+def denominators(hole, virt, pairs):
+    vmem = pl.BlockSpec(memory_space=pltpu.VMEM)
+    return pl.pallas_call(
+        denom_kernel,
+        out_shape=jax.ShapeDtypeStruct((ROWS, COLS), jnp.float32),
+        in_specs=[vmem] * 3,
+        out_specs=vmem,
+        compiler_params=pltpu.CompilerParams(vmem_limit_bytes=8 * MIB),
+    )(hole, virt, pairs)
+
+
+def final_kernel(t_ref, mine_ref, other_ref, denom_ref, token_ref, out_ref):
+    _, h, _ = here()
     exact = dict(precision=lax.Precision.HIGHEST, preferred_element_type=jnp.float32)
     row = lax.broadcasted_iota(jnp.int32, (128, COLS), 0)
     col = lax.broadcasted_iota(jnp.int32, (128, COLS), 1)
@@ -223,37 +254,19 @@
         goal = (row % 4) * VW + source * 4 + (row // 4) % 4
         put = jnp.where(col == goal, 1.0, 0.0)
         swapped += jnp.dot(t[dh * ROWS : (dh + 1) * ROWS], put, **exact)
-    own_a = ((y * 2 + h) * 2 + core) * 4 + col[:VW] // VW
-    pick_a = jnp.where(row[:VW] == own_a, 1.0, 0.0)
-    pick_b = jnp.where(row[:VW] == col[:VW] % VW, 1.0, 0.0)
-    virtual = jnp.broadcast_to(virt_ref[...], (8, VW))
-    virt_a = jnp.dot(virtual, pick_a, **exact)[:1]
-    virt_b = jnp.dot(virtual, pick_b, **exact)[:1]
-    count = hole_ref.shape[1]
-    orbital = lax.broadcasted_iota(jnp.int32, (count, ROWS), 0)
-    hole = jnp.broadcast_to(hole_ref[...], (8, count))
-    diagonal = lax.broadcasted_iota(jnp.int32, (ROWS, ROWS), 0) == lax.broadcasted_iota(
-        jnp.int32, (ROWS, ROWS), 1
-    )
-    holes = jnp.zeros((ROWS, 1), jnp.float32)
-    for k in range(2):
-        pick = jnp.where(orbital == pairs_ref[k : k + 1, :], 1.0, 0.0)
-        energy = jnp.dot(hole, pick, **exact)[:1]
-        holes += jnp.sum(jnp.where(diagonal, energy, 0.0), axis=1, keepdims=True)
-    denom = holes + virt_a + virt_b
     antisym = mine_ref[...] - swapped
-    out_ref[...] = -(other_ref[...].astype(jnp.float32) + 0.5 * antisym) / denom
-
-
-def final(t, mine, other_terms, hole, virt, pairs, token):
+    out_ref[...] = -(other_ref[...].astype(jnp.float32) + 0.5 * antisym) / denom_ref[...]
+
+
+def final(t, mine, other_terms, denom, token):
     vmem = pl.BlockSpec(memory_space=pltpu.VMEM)
     return pl.pallas_call(
         final_kernel,
         out_shape=jax.ShapeDtypeStruct((ROWS, COLS), jnp.float32),
-        in_specs=[vmem] * 6 + [pl.BlockSpec(memory_space=pl.ANY)],
+        in_specs=[vmem] * 4 + [pl.BlockSpec(memory_space=pl.ANY)],
         out_specs=vmem,
         compiler_params=pltpu.CompilerParams(vmem_limit_bytes=8 * MIB),
-    )(t, mine, other_terms, hole, virt, pairs, token)
+    )(t, mine, other_terms, denom, token)
 
 
 def group(kind):
@@ -302,7 +315,10 @@
     ints = jnp.transpose(after(integrals, g), (1, 0, 2))
     ints_own = lax.dynamic_slice_in_dim(ints, core * C_HALF, C_HALF, axis=1)
     ints_own = ints_own.reshape(K_ALL, COLS)
-    g = stage(g, zr1, ints_own, cost=COSTS[7])
+    denom = denominators(
+        after(hole_energy.reshape(1, -1), g), virtual_energy.reshape(1, -1), pair_orbitals.T
+    )
+    g = stage(g, zr1, ints_own, denom, cost=COSTS[7])
     zf1 = shift("zf1", after(zr1, g), dy=-1)
 
     near = {(0, 0, 0): own, (0, 0, 1): r0, (0, 0, 2): f0, (0, 0, 3): l0}
@@ -324,15 +340,7 @@
     direct, mixed = spread(by_z)
     swapped = exchange(mixed.reshape(8, 16, 128), "yc").reshape(128, 128)
 
-    return final(
-        swapped,
-        direct,
-        other_terms,
-        hole_energy.reshape(1, -1),
-        virtual_energy.reshape(1, -1),
-        pair_orbitals.T,
-        g,
-    )
+    return final(swapped, direct, other_terms, denom, g)
 
 
 def solution(mesh):

time: 126 us -> 125 us (level)
  no operation moved by 1% of the time
where the time goes in v4:
time: 125 us
  blocking collectives  46 us (37%)
  starting transfers between devices  38.3 us (31%)
  waiting for transfers between devices  30.2 us (24%)
  Pallas kernels  8.27 us (7%)
  local copies, waits for them, and re-layouts  1.9 us (2%)
    all_to_all x3, blocking collectives, exchange(): lax.all_to_all(value, ('bulk', 'occ'), 0, 0, axis_index_groups=group(kind...  46 us
    ppermute x18, starting transfers between devices, bulk_shift(): return lax.ppermute(value, 'bulk', pairs)  38.3 us
    ppermute x18, waiting for transfers between devices, bulk_shift(): return lax.ppermute(value, 'bulk', pairs)  30.2 us
    pallas_call x4, Pallas kernels, ladder(): pl.pallas_call(ladder_kernel, out_shape=jax.ShapeDtypeStruct((m, COLS), j...  4.76 us
  transfers between devices with their start and end apart: 18, of which 5 were waited for; matrix products, arithmetic and copies ran while one was open for 0% of the time, Pallas kernels for 3%

profile of v4, /device:TPU:1, one launch (start us, length us, event | category | flops | bytes accessed | tf_op | source)
XLA Modules:
  0.0 124.9 jit_solution(12916105887501789191)
XLA Ops:
  0.0 1.2 copy-done.4
  1.2 1.9 %shard_map.64 = (bf16[32,7200]{1,0:T(8,128)(2,1)S(1)}, bf16[32,7200]{1,0:T(8,128)(2,1)S(1)}, f32[8,128]{1,0:T(8,128)S(1)}) custom-call(bf16[32,16,900]{2,1,0:T(8,128)(2,1)S(1)} %copy-done.4), custom_call_target="tpu_custom_call" | custom-call | flops 471859200 | bytes 2097152 | tf_op jit(solution)/shard_map/pallas_call | solution.py:91
  3.1 3.3 %collective-permute-start.1 = (bf16[32,7200]{1,0:T(8,128)(2,1)S(1)}, bf16[32,7200]{1,0:T(8,128)(2,1)S(1)}, u32[]{:S(2)}, u32[]{:S(2)}) collective-permute-start(bf16[32,7200]{1,0:T(8,128)(2,1)S(1)} %get-tuple-element.32), channel_id=1, source_target_pairs={{0,16},{16,0},{32,48},{48,32},{64,80},{80,64},{96,112},{112,96},{1... | collective-permute-start | bytes 1382408 | tf_op jit(solution)/shard_map/sib/ppermute | solution.py:37
  6.4 1.0 collective-permute-start
  7.5 0.5 collective-permute-start.2
  7.9 6.4 %collective-permute-start.7 = (bf16[32,7200]{1,0:T(8,128)(2,1)S(1)}, bf16[32,7200]{1,0:T(8,128)(2,1)S(1)}, u32[]{:S(2)}, u32[]{:S(2)}) collective-permute-start(bf16[32,7200]{1,0:T(8,128)(2,1)S(1)} %get-tuple-element.30.refs_0_), channel_id=1, source_target_pairs={{0,32},{16,48},{32,0},{48,16},{64,96},{80,112},{96,64},{112,80},{1... | collective-permute-start | bytes 1382408 | tf_op jit(solution)/shard_map/z0/ppermute | solution.py:37
  14.5 2.7 %collective-permute-start.4 = (bf16[32,7200]{1,0:T(8,128)(2,1)S(1)}, bf16[32,7200]{1,0:T(8,128)(2,1)S(1)}, u32[]{:S(2)}, u32[]{:S(2)}) collective-permute-start(bf16[32,7200]{1,0:T(8,128)(2,1)S(1)} %collective-permute-done.1.refs_4_), channel_id=1, source_target_pairs={{0,192},{16,208},{32,224},{48,240},{64,0},{80,16},{96,32},{112,48}... | collective-permute-start | bytes 1382408 | tf_op jit(solution)/shard_map/r1/ppermute | solution.py:37
  17.2 1.5 %collective-permute-done.refs_1_ = bf16[32,7200]{1,0:T(8,128)(2,1)S(1)} collective-permute-done((bf16[32,7200]{1,0:T(8,128)(2,1)S(1)}, bf16[32,7200]{1,0:T(8,128)(2,1)S(1)}, u32[]{:S(2)}, u32[]{:S(2)}) %collective-permute-start) | collective-permute-done | bytes 460832 | tf_op jit(solution)/shard_map/r0/ppermute | solution.py:37
  18.7 5.7 %collective-permute-start.8 = (bf16[32,7200]{1,0:T(8,128)(2,1)S(1)}, bf16[32,7200]{1,0:T(8,128)(2,1)S(1)}, u32[]{:S(2)}, u32[]{:S(2)}) collective-permute-start(bf16[32,7200]{1,0:T(8,128)(2,1)S(1)} %collective-permute-done.1.refs_4_), channel_id=1, source_target_pairs={{0,32},{16,48},{32,0},{48,16},{64,96},{80,112},{96,64},{112,80},{1... | collective-permute-start | bytes 1382408 | tf_op jit(solution)/shard_map/z1/ppermute | solution.py:37
  24.4 0.2 dynamic-slice_bitcast_fusion
  24.7 1.7 %collective-permute-start.11 = (bf16[900,8,256]{2,1,0:T(8,128)(2,1)S(1)}, bf16[900,8,256]{2,1,0:T(8,128)(2,1)S(1)}, u32[]{:S(2)}, u32[]{:S(2)}) collective-permute-start(bf16[900,8,256]{2,1,0:T(8,128)(2,1)S(1)} %dynamic-slice_bitcast_fusion), channel_id=1, source_target_pairs={{0,16},{16,0},{32,48},{48,32},{64,80},{80,64},{96,112},{112,96},{1... | collective-permute-start | bytes 11059208 | tf_op jit(solution)/shard_map/ints/ppermute | solution.py:37
  26.4 4.2 %collective-permute-done.5.refs_7_ = bf16[32,7200]{1,0:T(8,128)(2,1)S(1)} collective-permute-done((bf16[32,7200]{1,0:T(8,128)(2,1)S(1)}, bf16[32,7200]{1,0:T(8,128)(2,1)S(1)}, u32[]{:S(2)}, u32[]{:S(2)}) %collective-permute-start.5) | collective-permute-done | bytes 460832 | tf_op jit(solution)/shard_map/l1/ppermute | solution.py:37
  30.6 1.5 %collective-permute-start.6 = (bf16[32,7200]{1,0:T(8,128)(2,1)S(1)}, bf16[32,7200]{1,0:T(8,128)(2,1)S(1)}, u32[]{:S(2)}, u32[]{:S(2)}) collective-permute-start(bf16[32,7200]{1,0:T(8,128)(2,1)S(1)} %collective-permute-done.5.refs_7_), channel_id=1, source_target_pairs={{0,64},{16,80},{32,96},{48,112},{64,128},{80,144},{96,160},{112,17... | collective-permute-start | bytes 1382408 | tf_op jit(solution)/shard_map/f1/ppermute | solution.py:37
  32.2 9.4 %collective-permute-done.3.refs_2_ = bf16[32,7200]{1,0:T(8,128)(2,1)S(1)} collective-permute-done((bf16[32,7200]{1,0:T(8,128)(2,1)S(1)}, bf16[32,7200]{1,0:T(8,128)(2,1)S(1)}, u32[]{:S(2)}, u32[]{:S(2)}) %collective-permute-start.3) | collective-permute-done | bytes 460832 | tf_op jit(solution)/shard_map/f0/ppermute | solution.py:37
  41.6 1.5 %collective-permute-start.9 = (bf16[32,7200]{1,0:T(8,128)(2,1)S(1)}, bf16[32,7200]{1,0:T(8,128)(2,1)S(1)}, u32[]{:S(2)}, u32[]{:S(2)}) collective-permute-start(bf16[32,7200]{1,0:T(8,128)(2,1)S(1)} %collective-permute-done.7.refs_0_), channel_id=1, source_target_pairs={{0,192},{16,208},{32,224},{48,240},{64,0},{80,16},{96,32},{112,48}... | collective-permute-start | bytes 1382408 | tf_op jit(solution)/shard_map/zr0/ppermute | solution.py:37
  43.2 1.4 %collective-permute-start.15 = (bf16[32,7200]{1,0:T(8,128)(2,1)S(1)}, bf16[32,7200]{1,0:T(8,128)(2,1)S(1)}, u32[]{:S(2)}, u32[]{:S(2)}) collective-permute-start(bf16[32,7200]{1,0:T(8,128)(2,1)S(1)} %collective-permute-done.8.refs_4_), channel_id=1, source_target_pairs={{0,64},{16,80},{32,96},{48,112},{64,128},{80,144},{96,160},{112,17... | collective-permute-start | bytes 1382408 | tf_op jit(solution)/shard_map/zl1/ppermute | solution.py:37
  44.6 8.3 %collective-permute-done.10.refs_3_ = bf16[32,7200]{1,0:T(8,128)(2,1)S(1)} collective-permute-done((bf16[32,7200]{1,0:T(8,128)(2,1)S(1)}, bf16[32,7200]{1,0:T(8,128)(2,1)S(1)}, u32[]{:S(2)}, u32[]{:S(2)}) %collective-permute-start.10) | collective-permute-done | bytes 460832 | tf_op jit(solution)/shard_map/zl0/ppermute | solution.py:37
  52.9 0.3 collective-permute-start.12
  53.6 0.3 shard_map.73.denom_ref
  53.9 6.7 %collective-permute-done.13.refs_5_ = bf16[32,7200]{1,0:T(8,128)(2,1)S(1)} collective-permute-done((bf16[32,7200]{1,0:T(8,128)(2,1)S(1)}, bf16[32,7200]{1,0:T(8,128)(2,1)S(1)}, u32[]{:S(2)}, u32[]{:S(2)}) %collective-permute-start.13) | collective-permute-done | bytes 460832 | tf_op jit(solution)/shard_map/zr1/ppermute | solution.py:37
  60.6 1.6 %collective-permute-start.14 = (bf16[32,7200]{1,0:T(8,128)(2,1)S(1)}, bf16[32,7200]{1,0:T(8,128)(2,1)S(1)}, u32[]{:S(2)}, u32[]{:S(2)}) collective-permute-start(bf16[32,7200]{1,0:T(8,128)(2,1)S(1)} %collective-permute-done.13.refs_5_), channel_id=1, source_target_pairs={{0,192},{16,208},{32,224},{48,240},{64,0},{80,16},{96,32},{112,48}... | collective-permute-start | bytes 1382408 | tf_op jit(solution)/shard_map/zf1/ppermute | solution.py:37
  62.2 1.2 shard_map.71
  63.4 6.5 %collective-permute-start.16 = (f32[256,256]{1,0:T(8,128)S(1)}, f32[256,256]{1,0:T(8,128)S(1)}, u32[]{:S(2)}, u32[]{:S(2)}) collective-permute-start(f32[256,256]{1,0:T(8,128)S(1)} %shard_map.71), channel_id=1, source_target_pairs={{0,16},{16,0},{32,48},{48,32},{64,80},{80,64},{96,112},{112,96},{1... | collective-permute-start | bytes 786440 | tf_op jit(solution)/shard_map/t0/ppermute | solution.py:37
  69.9 1.2 shard_map.72.refs_0_
  71.1 1.2 shard_map.75
  72.3 4.0 %collective-permute-start.17 = (f32[256,256]{1,0:T(8,128)S(1)}, f32[256,256]{1,0:T(8,128)S(1)}, u32[]{:S(2)}, u32[]{:S(2)}) collective-permute-start(f32[256,256]{1,0:T(8,128)S(1)} %shard_map.75), channel_id=1, source_target_pairs={{0,16},{16,0},{32,48},{48,32},{64,80},{80,64},{96,112},{112,96},{1... | collective-permute-start | bytes 786440 | tf_op jit(solution)/shard_map/t1/ppermute | solution.py:37
  76.3 1.2 shard_map.76.refs_1_
  77.6 12.5 %all_to_all.15 = f32[4,4,32,256]{3,2,1,0:T(8,128)S(1)} all-to-all(f32[4,4,32,256]{3,2,1,0:T(8,128)S(1)} %shard_map.77), channel_id=1, replica_groups={{0,4,8,12},{1,5,9,13},{2,6,10,14},{3,7,11,15},{16,20,24,28},{17,21,25,2..., dimensions={0} | all-to-all | bytes 1048576 | tf_op jit(solution)/shard_map/all_to_all | solution.py:283
  90.2 21.7 %all_to_all.16.t_ref = f32[8,32,256]{2,1,0:T(8,128)S(1)} all-to-all(f32[8,32,256]{2,1,0:T(8,128)S(1)} %bitcast.22), channel_id=1, replica_groups={{0,1,2,3,32,33,34,35},{4,5,6,7,36,37,38,39},{8,9,10,11,40,41,42,43},{12..., dimensions={0} | all-to-all | bytes 524288 | tf_op jit(solution)/shard_map/all_to_all | solution.py:283
  111.9 0.3 shard_map.78
  112.2 11.7 %all_to_all.17 = f32[8,16,128]{2,1,0:T(8,128)S(1)} all-to-all(f32[8,16,128]{2,1,0:T(8,128)S(1)} %bitcast.16), channel_id=1, replica_groups={{0,16,64,80,128,144,192,208},{1,17,65,81,129,145,193,209},{2,18,66,82,1..., dimensions={0} | all-to-all | bytes 131072 | tf_op jit(solution)/shard_map/all_to_all | solution.py:283
  123.9 1.0 shard_map.79
  (42 shorter events, 0.9 us)
Async XLA Ops:
  0.0 1.2 copy-start.4
  3.1 11.3 %collective-permute-start.1 = (bf16[32,7200]{1,0:T(8,128)(2,1)S(1)}, bf16[32,7200]{1,0:T(8,128)(2,1)S(1)}, u32[]{:S(2)}, u32[]{:S(2)}) collective-permute-start(bf16[32,7200]{1,0:T(8,128)(2,1)S(1)} %get-tuple-element.32), channel_id=1, source_target_pairs={{0,16},{16,0},{32,48},{48,32},{64,80},{80,64},{96,112},{112,96},{1... | collective-permute-start | bytes 1382408 | tf_op jit(solution)/shard_map/sib/ppermute | solution.py:37
  6.4 12.3 %collective-permute-start = (bf16[32,7200]{1,0:T(8,128)(2,1)S(1)}, bf16[32,7200]{1,0:T(8,128)(2,1)S(1)}, u32[]{:S(2)}, u32[]{:S(2)}) collective-permute-start(bf16[32,7200]{1,0:T(8,128)(2,1)S(1)} %get-tuple-element.30.refs_0_), channel_id=1, source_target_pairs={{0,192},{16,208},{32,224},{48,240},{64,0},{80,16},{96,32},{112,48}... | collective-permute-start | bytes 1382408 | tf_op jit(solution)/shard_map/r0/ppermute | solution.py:37
  7.5 17.0 %collective-permute-start.2 = (bf16[32,7200]{1,0:T(8,128)(2,1)S(1)}, bf16[32,7200]{1,0:T(8,128)(2,1)S(1)}, u32[]{:S(2)}, u32[]{:S(2)}) collective-permute-start(bf16[32,7200]{1,0:T(8,128)(2,1)S(1)} %get-tuple-element.30.refs_0_), channel_id=1, source_target_pairs={{0,64},{16,80},{32,96},{48,112},{64,128},{80,144},{96,160},{112,17... | collective-permute-start | bytes 1382408 | tf_op jit(solution)/shard_map/l0/ppermute | solution.py:37
  7.9 24.1 %collective-permute-start.7 = (bf16[32,7200]{1,0:T(8,128)(2,1)S(1)}, bf16[32,7200]{1,0:T(8,128)(2,1)S(1)}, u32[]{:S(2)}, u32[]{:S(2)}) collective-permute-start(bf16[32,7200]{1,0:T(8,128)(2,1)S(1)} %get-tuple-element.30.refs_0_), channel_id=1, source_target_pairs={{0,32},{16,48},{32,0},{48,16},{64,96},{80,112},{96,64},{112,80},{1... | collective-permute-start | bytes 1382408 | tf_op jit(solution)/shard_map/z0/ppermute | solution.py:37
  14.4 10.0 %slice-start = ((s8[7372800]{0:T(1024)(128)(4,1)}), s8[4194304]{0:T(1024)(128)(4,1)S(1)}, s32[]{:S(2)}) async-start(s8[7372800]{0:T(1024)(128)(4,1)} %bitcast.20), calls=%async_computation.3 | async-start | bytes 8388608
  14.4 10.0 %slice-start.1 = ((s8[7372800]{0:T(1024)(128)(4,1)}), s8[3178496]{0:T(1024)(128)(4,1)S(1)}, s32[]{:S(2)}) async-start(s8[7372800]{0:T(1024)(128)(4,1)} %bitcast.20), calls=%async_computation.4 | async-start | bytes 6356992
  14.4 16.2 %collective-permute-start.5 = (bf16[32,7200]{1,0:T(8,128)(2,1)S(1)}, bf16[32,7200]{1,0:T(8,128)(2,1)S(1)}, u32[]{:S(2)}, u32[]{:S(2)}) collective-permute-start(bf16[32,7200]{1,0:T(8,128)(2,1)S(1)} %collective-permute-done.1.refs_4_), channel_id=1, source_target_pairs={{0,64},{16,80},{32,96},{48,112},{64,128},{80,144},{96,160},{112,17... | collective-permute-start | bytes 1382408 | tf_op jit(solution)/shard_map/l1/ppermute | solution.py:37
  14.5 16.1 %collective-permute-start.4 = (bf16[32,7200]{1,0:T(8,128)(2,1)S(1)}, bf16[32,7200]{1,0:T(8,128)(2,1)S(1)}, u32[]{:S(2)}, u32[]{:S(2)}) collective-permute-start(bf16[32,7200]{1,0:T(8,128)(2,1)S(1)} %collective-permute-done.1.refs_4_), channel_id=1, source_target_pairs={{0,192},{16,208},{32,224},{48,240},{64,0},{80,16},{96,32},{112,48}... | collective-permute-start | bytes 1382408 | tf_op jit(solution)/shard_map/r1/ppermute | solution.py:37
  18.7 24.4 %collective-permute-start.8 = (bf16[32,7200]{1,0:T(8,128)(2,1)S(1)}, bf16[32,7200]{1,0:T(8,128)(2,1)S(1)}, u32[]{:S(2)}, u32[]{:S(2)}) collective-permute-start(bf16[32,7200]{1,0:T(8,128)(2,1)S(1)} %collective-permute-done.1.refs_4_), channel_id=1, source_target_pairs={{0,32},{16,48},{32,0},{48,16},{64,96},{80,112},{96,64},{112,80},{1... | collective-permute-start | bytes 1382408 | tf_op jit(solution)/shard_map/z1/ppermute | solution.py:37
  24.7 37.5 %collective-permute-start.11 = (bf16[900,8,256]{2,1,0:T(8,128)(2,1)S(1)}, bf16[900,8,256]{2,1,0:T(8,128)(2,1)S(1)}, u32[]{:S(2)}, u32[]{:S(2)}) collective-permute-start(bf16[900,8,256]{2,1,0:T(8,128)(2,1)S(1)} %dynamic-slice_bitcast_fusion), channel_id=1, source_target_pairs={{0,16},{16,0},{32,48},{48,32},{64,80},{80,64},{96,112},{112,96},{1... | collective-permute-start | bytes 11059208 | tf_op jit(solution)/shard_map/ints/ppermute | solution.py:37
  30.6 11.0 %collective-permute-start.3 = (bf16[32,7200]{1,0:T(8,128)(2,1)S(1)}, bf16[32,7200]{1,0:T(8,128)(2,1)S(1)}, u32[]{:S(2)}, u32[]{:S(2)}) collective-permute-start(bf16[32,7200]{1,0:T(8,128)(2,1)S(1)} %collective-permute-done.refs_1_), channel_id=1, source_target_pairs={{0,192},{16,208},{32,224},{48,240},{64,0},{80,16},{96,32},{112,48}... | collective-permute-start | bytes 1382408 | tf_op jit(solution)/shard_map/f0/ppermute | solution.py:37
  30.6 12.5 %collective-permute-start.6 = (bf16[32,7200]{1,0:T(8,128)(2,1)S(1)}, bf16[32,7200]{1,0:T(8,128)(2,1)S(1)}, u32[]{:S(2)}, u32[]{:S(2)}) collective-permute-start(bf16[32,7200]{1,0:T(8,128)(2,1)S(1)} %collective-permute-done.5.refs_7_), channel_id=1, source_target_pairs={{0,64},{16,80},{32,96},{48,112},{64,128},{80,144},{96,160},{112,17... | collective-permute-start | bytes 1382408 | tf_op jit(solution)/shard_map/f1/ppermute | solution.py:37
  32.1 20.8 %collective-permute-start.10 = (bf16[32,7200]{1,0:T(8,128)(2,1)S(1)}, bf16[32,7200]{1,0:T(8,128)(2,1)S(1)}, u32[]{:S(2)}, u32[]{:S(2)}) collective-permute-start(bf16[32,7200]{1,0:T(8,128)(2,1)S(1)} %collective-permute-done.7.refs_0_), channel_id=1, source_target_pairs={{0,64},{16,80},{32,96},{48,112},{64,128},{80,144},{96,160},{112,17... | collective-permute-start | bytes 1382408 | tf_op jit(solution)/shard_map/zl0/ppermute | solution.py:37
  41.6 11.3 %collective-permute-start.9 = (bf16[32,7200]{1,0:T(8,128)(2,1)S(1)}, bf16[32,7200]{1,0:T(8,128)(2,1)S(1)}, u32[]{:S(2)}, u32[]{:S(2)}) collective-permute-start(bf16[32,7200]{1,0:T(8,128)(2,1)S(1)} %collective-permute-done.7.refs_0_), channel_id=1, source_target_pairs={{0,192},{16,208},{32,224},{48,240},{64,0},{80,16},{96,32},{112,48}... | collective-permute-start | bytes 1382408 | tf_op jit(solution)/shard_map/zr0/ppermute | solution.py:37
  43.1 17.5 %collective-permute-start.13 = (bf16[32,7200]{1,0:T(8,128)(2,1)S(1)}, bf16[32,7200]{1,0:T(8,128)(2,1)S(1)}, u32[]{:S(2)}, u32[]{:S(2)}) collective-permute-start(bf16[32,7200]{1,0:T(8,128)(2,1)S(1)} %collective-permute-done.8.refs_4_), channel_id=1, source_target_pairs={{0,192},{16,208},{32,224},{48,240},{64,0},{80,16},{96,32},{112,48}... | collective-permute-start | bytes 1382408 | tf_op jit(solution)/shard_map/zr1/ppermute | solution.py:37
  43.2 27.9 %collective-permute-start.15 = (bf16[32,7200]{1,0:T(8,128)(2,1)S(1)}, bf16[32,7200]{1,0:T(8,128)(2,1)S(1)}, u32[]{:S(2)}, u32[]{:S(2)}) collective-permute-start(bf16[32,7200]{1,0:T(8,128)(2,1)S(1)} %collective-permute-done.8.refs_4_), channel_id=1, source_target_pairs={{0,64},{16,80},{32,96},{48,112},{64,128},{80,144},{96,160},{112,17... | collective-permute-start | bytes 1382408 | tf_op jit(solution)/shard_map/zl1/ppermute | solution.py:37
  52.9 0.7 copy-start.1
  52.9 0.7 copy-start.2
  52.9 0.7 copy-start.3
  52.9 18.2 %collective-permute-start.12 = (bf16[32,7200]{1,0:T(8,128)(2,1)S(1)}, bf16[32,7200]{1,0:T(8,128)(2,1)S(1)}, u32[]{:S(2)}, u32[]{:S(2)}) collective-permute-start(bf16[32,7200]{1,0:T(8,128)(2,1)S(1)} %collective-permute-done.10.refs_3_), channel_id=1, source_target_pairs={{0,64},{16,80},{32,96},{48,112},{64,128},{80,144},{96,160},{112,17... | collective-permute-start | bytes 1382408 | tf_op jit(solution)/shard_map/zf0/ppermute | solution.py:37
  60.6 10.5 %collective-permute-start.14 = (bf16[32,7200]{1,0:T(8,128)(2,1)S(1)}, bf16[32,7200]{1,0:T(8,128)(2,1)S(1)}, u32[]{:S(2)}, u32[]{:S(2)}) collective-permute-start(bf16[32,7200]{1,0:T(8,128)(2,1)S(1)} %collective-permute-done.13.refs_5_), channel_id=1, source_target_pairs={{0,192},{16,208},{32,224},{48,240},{64,0},{80,16},{96,32},{112,48}... | collective-permute-start | bytes 1382408 | tf_op jit(solution)/shard_map/zf1/ppermute | solution.py:37
  63.4 7.7 %collective-permute-start.16 = (f32[256,256]{1,0:T(8,128)S(1)}, f32[256,256]{1,0:T(8,128)S(1)}, u32[]{:S(2)}, u32[]{:S(2)}) collective-permute-start(f32[256,256]{1,0:T(8,128)S(1)} %shard_map.71), channel_id=1, source_target_pairs={{0,16},{16,0},{32,48},{48,32},{64,80},{80,64},{96,112},{112,96},{1... | collective-permute-start | bytes 786440 | tf_op jit(solution)/shard_map/t0/ppermute | solution.py:37
  72.3 5.2 %collective-permute-start.17 = (f32[256,256]{1,0:T(8,128)S(1)}, f32[256,256]{1,0:T(8,128)S(1)}, u32[]{:S(2)}, u32[]{:S(2)}) collective-permute-start(f32[256,256]{1,0:T(8,128)S(1)} %shard_map.75), channel_id=1, source_target_pairs={{0,16},{16,0},{32,48},{48,32},{64,80},{80,64},{96,112},{112,96},{1... | collective-permute-start | bytes 786440 | tf_op jit(solution)/shard_map/t1/ppermute | solution.py:37
  77.5 46.4 %copy-start = (bf16[32,256]{1,0:T(8,128)(2,1)S(1)}, bf16[32,256]{1,0:T(8,128)(2,1)}, u32[]{:S(2)}) copy-start(bf16[32,256]{1,0:T(8,128)(2,1)} %other_ref.1) | copy-start | bytes 49156

commit v5 on v4

--- a/solution.py
+++ b/solution.py
@@ -177,19 +177,22 @@
         first = ((h + dh) % 2) * 4
         parts.append(t_ref[first] + t_ref[first + 1] + t_ref[first + 2] + t_ref[first + 3])
     here_ref[...] = parts[0]
-    both = jnp.concatenate(parts + [jnp.zeros((2 * ROWS, COLS), jnp.float32)], axis=0)
-    row = lax.broadcasted_iota(jnp.int32, (128, COLS), 0)
-    col = lax.broadcasted_iota(jnp.int32, (128, COLS), 1)
-    target = ((row // 32) * 2 + h) * 2 + (row // 16) % 2
-    want = ((row // 4) % 4) * VW + target * 4 + row % 4
-    pick = jnp.where(col == want, 1.0, 0.0)
-    out_ref[...] = lax.dot_general(
-        pick,
-        both,
-        (((1,), (1,)), ((), ())),
-        precision=lax.Precision.HIGHEST,
-        preferred_element_type=jnp.float32,
-    )
+    both = jnp.concatenate(parts, axis=0)
+    none = jnp.zeros_like(both)
+    row = lax.broadcasted_iota(jnp.int32, (64, COLS), 0)
+    col = lax.broadcasted_iota(jnp.int32, (64, COLS), 1)
+    target = ((row // 16) * 2 + h) * 2 + (row // 8) % 2
+    total = jnp.zeros((64, 128), jnp.float32)
+    for half in range(2):
+        want = (half * 2 + (row // 4) % 2) * VW + target * 4 + row % 4
+        total += lax.dot_general(
+            jnp.where(col == want, 1.0, 0.0),
+            jnp.concatenate([none, both] if half else [both, none], axis=0),
+            (((1,), (1,)), ((), ())),
+            precision=lax.Precision.HIGHEST,
+            preferred_element_type=jnp.float32,
+        )
+    out_ref[...] = total
 
 
 def spread(t):
@@ -198,7 +201,7 @@
         spread_kernel,
         out_shape=[
             jax.ShapeDtypeStruct((ROWS, COLS), jnp.float32),
-            jax.ShapeDtypeStruct((128, 128), jnp.float32),
+            jax.ShapeDtypeStruct((64, 128), jnp.float32),
         ],
         in_specs=[vmem],
         out_specs=[vmem] * 2,
@@ -245,15 +248,17 @@
 def final_kernel(t_ref, mine_ref, other_ref, denom_ref, token_ref, out_ref):
     _, h, _ = here()
     exact = dict(precision=lax.Precision.HIGHEST, preferred_element_type=jnp.float32)
-    row = lax.broadcasted_iota(jnp.int32, (128, COLS), 0)
-    col = lax.broadcasted_iota(jnp.int32, (128, COLS), 1)
+    row = lax.broadcasted_iota(jnp.int32, (64, COLS), 0)
+    col = lax.broadcasted_iota(jnp.int32, (64, COLS), 1)
     swapped = jnp.zeros((ROWS, COLS), jnp.float32)
     t = t_ref[...].T
-    for dh in range(2):
-        source = ((row // 32) * 2 + (h + dh) % 2) * 2 + (row // 16) % 2
-        goal = (row % 4) * VW + source * 4 + (row // 4) % 4
-        put = jnp.where(col == goal, 1.0, 0.0)
-        swapped += jnp.dot(t[dh * ROWS : (dh + 1) * ROWS], put, **exact)
+    for half in range(2):
+        for dh in range(2):
+            source = ((row // 16) * 2 + (h + dh) % 2) * 2 + (row // 8) % 2
+            goal = (row % 4) * VW + source * 4 + half * 2 + (row // 4) % 2
+            put = jnp.where(col == goal, 1.0, 0.0)
+            first = (half * 2 + dh) * ROWS
+            swapped += jnp.dot(t[first : first + ROWS], put, **exact)
     antisym = mine_ref[...] - swapped
     out_ref[...] = -(other_ref[...].astype(jnp.float32) + 0.5 * antisym) / denom_ref[...]
 
@@ -304,10 +309,10 @@
     ints_sib = shift("ints", ints_other, dc=1).reshape(K_ALL, COLS)
     g = stage(g, r1, l1, cost=COSTS[3])
     f1 = shift("f1", after(l1, g), dy=1)
-    g = stage(g, z0, cost=COSTS[4])
+    g = stage(g, z0, f0, cost=COSTS[4])
     zr0 = shift("zr0", after(z0, g), dy=-1)
     zl0 = shift("zl0", after(z0, g), dy=1)
-    g = stage(g, z1, f0, f1, cost=COSTS[5])
+    g = stage(g, z1, f1, cost=COSTS[5])
     zr1 = shift("zr1", after(z1, g), dy=-1)
     zl1 = shift("zl1", after(z1, g), dy=1)
     g = stage(g, zr0, zl0, cost=COSTS[6])
@@ -338,7 +343,7 @@
     by_z = jnp.broadcast_to(rows_x[None], (2,) + rows_x.shape).reshape(8, ROWS, COLS)
     by_z = exchange(by_z, "hz")
     direct, mixed = spread(by_z)
-    swapped = exchange(mixed.reshape(8, 16, 128), "yc").reshape(128, 128)
+    swapped = exchange(mixed.reshape(8, 8, 128), "yc").reshape(64, 128)
 
     return final(swapped, direct, other_terms, denom, g)
 

time: 125 us -> 125 us (level)
  starting transfers between devices: 38.3 us -> 39.8 us
    ppermute x18, starting transfers between devices: 38.3 us -> 39.8 us  [bulk_shift(): return lax.ppermute(value, 'bulk', pairs)]
where the time goes in v5:
time: 125 us
  blocking collectives  44.9 us (36%)
  starting transfers between devices  39.8 us (32%)
  waiting for transfers between devices  29.6 us (24%)
  Pallas kernels  8.29 us (7%)
  local copies, waits for them, and re-layouts  1.9 us (2%)
    all_to_all x3, blocking collectives, exchange(): lax.all_to_all(value, ('bulk', 'occ'), 0, 0, axis_index_groups=group(kind...  44.9 us
    ppermute x18, starting transfers between devices, bulk_shift(): return lax.ppermute(value, 'bulk', pairs)  39.8 us
    ppermute x18, waiting for transfers between devices, bulk_shift(): return lax.ppermute(value, 'bulk', pairs)  29.6 us
    pallas_call x4, Pallas kernels, ladder(): pl.pallas_call(ladder_kernel, out_shape=jax.ShapeDtypeStruct((m, COLS), j...  4.76 us
  transfers between devices with their start and end apart: 18, of which 5 were waited for; matrix products, arithmetic and copies ran while one was open for 0% of the time, Pallas kernels for 3%

profile of v5, /device:TPU:1, one launch (start us, length us, event | category | flops | bytes accessed | tf_op | source)
XLA Modules:
  0.0 124.8 jit_solution(6785886759861076130)
XLA Ops:
  0.0 1.2 copy-done.4
  1.2 1.9 %shard_map.64 = (bf16[32,7200]{1,0:T(8,128)(2,1)S(1)}, bf16[32,7200]{1,0:T(8,128)(2,1)S(1)}, f32[8,128]{1,0:T(8,128)S(1)}) custom-call(bf16[32,16,900]{2,1,0:T(8,128)(2,1)S(1)} %copy-done.4), custom_call_target="tpu_custom_call" | custom-call | flops 471859200 | bytes 2097152 | tf_op jit(solution)/shard_map/pallas_call | solution.py:91
  3.1 3.3 %collective-permute-start.1 = (bf16[32,7200]{1,0:T(8,128)(2,1)S(1)}, bf16[32,7200]{1,0:T(8,128)(2,1)S(1)}, u32[]{:S(2)}, u32[]{:S(2)}) collective-permute-start(bf16[32,7200]{1,0:T(8,128)(2,1)S(1)} %get-tuple-element.32), channel_id=1, source_target_pairs={{0,16},{16,0},{32,48},{48,32},{64,80},{80,64},{96,112},{112,96},{1... | collective-permute-start | bytes 1382408 | tf_op jit(solution)/shard_map/sib/ppermute | solution.py:37
  6.4 1.0 collective-permute-start
  7.5 0.5 collective-permute-start.2
  7.9 6.4 %collective-permute-start.7 = (bf16[32,7200]{1,0:T(8,128)(2,1)S(1)}, bf16[32,7200]{1,0:T(8,128)(2,1)S(1)}, u32[]{:S(2)}, u32[]{:S(2)}) collective-permute-start(bf16[32,7200]{1,0:T(8,128)(2,1)S(1)} %get-tuple-element.30.refs_0_), channel_id=1, source_target_pairs={{0,32},{16,48},{32,0},{48,16},{64,96},{80,112},{96,64},{112,80},{1... | collective-permute-start | bytes 1382408 | tf_op jit(solution)/shard_map/z0/ppermute | solution.py:37
  14.5 2.7 %collective-permute-start.4 = (bf16[32,7200]{1,0:T(8,128)(2,1)S(1)}, bf16[32,7200]{1,0:T(8,128)(2,1)S(1)}, u32[]{:S(2)}, u32[]{:S(2)}) collective-permute-start(bf16[32,7200]{1,0:T(8,128)(2,1)S(1)} %collective-permute-done.1.refs_4_), channel_id=1, source_target_pairs={{0,192},{16,208},{32,224},{48,240},{64,0},{80,16},{96,32},{112,48}... | collective-permute-start | bytes 1382408 | tf_op jit(solution)/shard_map/r1/ppermute | solution.py:37
  17.2 1.5 %collective-permute-done.refs_1_ = bf16[32,7200]{1,0:T(8,128)(2,1)S(1)} collective-permute-done((bf16[32,7200]{1,0:T(8,128)(2,1)S(1)}, bf16[32,7200]{1,0:T(8,128)(2,1)S(1)}, u32[]{:S(2)}, u32[]{:S(2)}) %collective-permute-start) | collective-permute-done | bytes 460832 | tf_op jit(solution)/shard_map/r0/ppermute | solution.py:37
  18.7 5.7 %collective-permute-start.8 = (bf16[32,7200]{1,0:T(8,128)(2,1)S(1)}, bf16[32,7200]{1,0:T(8,128)(2,1)S(1)}, u32[]{:S(2)}, u32[]{:S(2)}) collective-permute-start(bf16[32,7200]{1,0:T(8,128)(2,1)S(1)} %collective-permute-done.1.refs_4_), channel_id=1, source_target_pairs={{0,32},{16,48},{32,0},{48,16},{64,96},{80,112},{96,64},{112,80},{1... | collective-permute-start | bytes 1382408 | tf_op jit(solution)/shard_map/z1/ppermute | solution.py:37
  24.7 1.7 %collective-permute-start.11 = (bf16[900,8,256]{2,1,0:T(8,128)(2,1)S(1)}, bf16[900,8,256]{2,1,0:T(8,128)(2,1)S(1)}, u32[]{:S(2)}, u32[]{:S(2)}) collective-permute-start(bf16[900,8,256]{2,1,0:T(8,128)(2,1)S(1)} %dynamic-slice_bitcast_fusion), channel_id=1, source_target_pairs={{0,16},{16,0},{32,48},{48,32},{64,80},{80,64},{96,112},{112,96},{1... | collective-permute-start | bytes 11059208 | tf_op jit(solution)/shard_map/ints/ppermute | solution.py:37
  26.4 4.2 %collective-permute-done.5.refs_7_ = bf16[32,7200]{1,0:T(8,128)(2,1)S(1)} collective-permute-done((bf16[32,7200]{1,0:T(8,128)(2,1)S(1)}, bf16[32,7200]{1,0:T(8,128)(2,1)S(1)}, u32[]{:S(2)}, u32[]{:S(2)}) %collective-permute-start.5) | collective-permute-done | bytes 460832 | tf_op jit(solution)/shard_map/l1/ppermute | solution.py:37
  30.6 1.5 %collective-permute-start.6 = (bf16[32,7200]{1,0:T(8,128)(2,1)S(1)}, bf16[32,7200]{1,0:T(8,128)(2,1)S(1)}, u32[]{:S(2)}, u32[]{:S(2)}) collective-permute-start(bf16[32,7200]{1,0:T(8,128)(2,1)S(1)} %collective-permute-done.5.refs_7_), channel_id=1, source_target_pairs={{0,64},{16,80},{32,96},{48,112},{64,128},{80,144},{96,160},{112,17... | collective-permute-start | bytes 1382408 | tf_op jit(solution)/shard_map/f1/ppermute | solution.py:37
  32.1 9.5 %collective-permute-done.3.refs_2_ = bf16[32,7200]{1,0:T(8,128)(2,1)S(1)} collective-permute-done((bf16[32,7200]{1,0:T(8,128)(2,1)S(1)}, bf16[32,7200]{1,0:T(8,128)(2,1)S(1)}, u32[]{:S(2)}, u32[]{:S(2)}) %collective-permute-start.3) | collective-permute-done | bytes 460832 | tf_op jit(solution)/shard_map/f0/ppermute | solution.py:37
  41.6 2.7 %collective-permute-start.9 = (bf16[32,7200]{1,0:T(8,128)(2,1)S(1)}, bf16[32,7200]{1,0:T(8,128)(2,1)S(1)}, u32[]{:S(2)}, u32[]{:S(2)}) collective-permute-start(bf16[32,7200]{1,0:T(8,128)(2,1)S(1)} %collective-permute-done.7.refs_0_), channel_id=1, source_target_pairs={{0,192},{16,208},{32,224},{48,240},{64,0},{80,16},{96,32},{112,48}... | collective-permute-start | bytes 1382408 | tf_op jit(solution)/shard_map/zr0/ppermute | solution.py:37
  44.3 0.3 collective-permute-start.13
  44.6 1.2 collective-permute-start.15
  45.8 7.1 %collective-permute-done.10.refs_3_ = bf16[32,7200]{1,0:T(8,128)(2,1)S(1)} collective-permute-done((bf16[32,7200]{1,0:T(8,128)(2,1)S(1)}, bf16[32,7200]{1,0:T(8,128)(2,1)S(1)}, u32[]{:S(2)}, u32[]{:S(2)}) %collective-permute-start.10) | collective-permute-done | bytes 460832 | tf_op jit(solution)/shard_map/zl0/ppermute | solution.py:37
  52.9 0.3 collective-permute-start.12
  53.6 0.3 shard_map.73.denom_ref
  53.9 7.2 %collective-permute-done.13.refs_5_ = bf16[32,7200]{1,0:T(8,128)(2,1)S(1)} collective-permute-done((bf16[32,7200]{1,0:T(8,128)(2,1)S(1)}, bf16[32,7200]{1,0:T(8,128)(2,1)S(1)}, u32[]{:S(2)}, u32[]{:S(2)}) %collective-permute-start.13) | collective-permute-done | bytes 460832 | tf_op jit(solution)/shard_map/zr1/ppermute | solution.py:37
  61.1 3.4 %collective-permute-start.14 = (bf16[32,7200]{1,0:T(8,128)(2,1)S(1)}, bf16[32,7200]{1,0:T(8,128)(2,1)S(1)}, u32[]{:S(2)}, u32[]{:S(2)}) collective-permute-start(bf16[32,7200]{1,0:T(8,128)(2,1)S(1)} %collective-permute-done.13.refs_5_), channel_id=1, source_target_pairs={{0,192},{16,208},{32,224},{48,240},{64,0},{80,16},{96,32},{112,48}... | collective-permute-start | bytes 1382408 | tf_op jit(solution)/shard_map/zf1/ppermute | solution.py:37
  64.5 1.2 shard_map.71
  65.7 4.4 %collective-permute-start.16 = (f32[256,256]{1,0:T(8,128)S(1)}, f32[256,256]{1,0:T(8,128)S(1)}, u32[]{:S(2)}, u32[]{:S(2)}) collective-permute-start(f32[256,256]{1,0:T(8,128)S(1)} %shard_map.71), channel_id=1, source_target_pairs={{0,16},{16,0},{32,48},{48,32},{64,80},{80,64},{96,112},{112,96},{1... | collective-permute-start | bytes 786440 | tf_op jit(solution)/shard_map/t0/ppermute | solution.py:37
  70.2 1.2 shard_map.72.refs_0_
  71.4 1.2 shard_map.75
  72.6 4.6 %collective-permute-start.17 = (f32[256,256]{1,0:T(8,128)S(1)}, f32[256,256]{1,0:T(8,128)S(1)}, u32[]{:S(2)}, u32[]{:S(2)}) collective-permute-start(f32[256,256]{1,0:T(8,128)S(1)} %shard_map.75), channel_id=1, source_target_pairs={{0,16},{16,0},{32,48},{48,32},{64,80},{80,64},{96,112},{112,96},{1... | collective-permute-start | bytes 786440 | tf_op jit(solution)/shard_map/t1/ppermute | solution.py:37
  77.2 1.2 shard_map.76.refs_1_
  78.5 12.5 %all_to_all.15 = f32[4,4,32,256]{3,2,1,0:T(8,128)S(1)} all-to-all(f32[4,4,32,256]{3,2,1,0:T(8,128)S(1)} %shard_map.77), channel_id=1, replica_groups={{0,4,8,12},{1,5,9,13},{2,6,10,14},{3,7,11,15},{16,20,24,28},{17,21,25,2..., dimensions={0} | all-to-all | bytes 1048576 | tf_op jit(solution)/shard_map/all_to_all | solution.py:288
  91.1 20.8 %all_to_all.16.t_ref = f32[8,32,256]{2,1,0:T(8,128)S(1)} all-to-all(f32[8,32,256]{2,1,0:T(8,128)S(1)} %bitcast.22), channel_id=1, replica_groups={{0,1,2,3,32,33,34,35},{4,5,6,7,36,37,38,39},{8,9,10,11,40,41,42,43},{12..., dimensions={0} | all-to-all | bytes 524288 | tf_op jit(solution)/shard_map/all_to_all | solution.py:288
  111.9 0.3 shard_map.78
  112.2 11.6 %all_to_all.17 = f32[8,8,128]{2,1,0:T(8,128)S(1)} all-to-all(f32[8,8,128]{2,1,0:T(8,128)S(1)} %bitcast.16), channel_id=1, replica_groups={{0,16,64,80,128,144,192,208},{1,17,65,81,129,145,193,209},{2,18,66,82,1..., dimensions={0} | all-to-all | bytes 65536 | tf_op jit(solution)/shard_map/all_to_all | solution.py:288
  123.8 0.9 shard_map.79
  (42 shorter events, 1.0 us)
Async XLA Ops:
  0.0 1.2 copy-start.4
  3.1 11.3 %collective-permute-start.1 = (bf16[32,7200]{1,0:T(8,128)(2,1)S(1)}, bf16[32,7200]{1,0:T(8,128)(2,1)S(1)}, u32[]{:S(2)}, u32[]{:S(2)}) collective-permute-start(bf16[32,7200]{1,0:T(8,128)(2,1)S(1)} %get-tuple-element.32), channel_id=1, source_target_pairs={{0,16},{16,0},{32,48},{48,32},{64,80},{80,64},{96,112},{112,96},{1... | collective-permute-start | bytes 1382408 | tf_op jit(solution)/shard_map/sib/ppermute | solution.py:37
  6.4 12.3 %collective-permute-start = (bf16[32,7200]{1,0:T(8,128)(2,1)S(1)}, bf16[32,7200]{1,0:T(8,128)(2,1)S(1)}, u32[]{:S(2)}, u32[]{:S(2)}) collective-permute-start(bf16[32,7200]{1,0:T(8,128)(2,1)S(1)} %get-tuple-element.30.refs_0_), channel_id=1, source_target_pairs={{0,192},{16,208},{32,224},{48,240},{64,0},{80,16},{96,32},{112,48}... | collective-permute-start | bytes 1382408 | tf_op jit(solution)/shard_map/r0/ppermute | solution.py:37
  7.5 17.0 %collective-permute-start.2 = (bf16[32,7200]{1,0:T(8,128)(2,1)S(1)}, bf16[32,7200]{1,0:T(8,128)(2,1)S(1)}, u32[]{:S(2)}, u32[]{:S(2)}) collective-permute-start(bf16[32,7200]{1,0:T(8,128)(2,1)S(1)} %get-tuple-element.30.refs_0_), channel_id=1, source_target_pairs={{0,64},{16,80},{32,96},{48,112},{64,128},{80,144},{96,160},{112,17... | collective-permute-start | bytes 1382408 | tf_op jit(solution)/shard_map/l0/ppermute | solution.py:37
  7.9 24.1 %collective-permute-start.7 = (bf16[32,7200]{1,0:T(8,128)(2,1)S(1)}, bf16[32,7200]{1,0:T(8,128)(2,1)S(1)}, u32[]{:S(2)}, u32[]{:S(2)}) collective-permute-start(bf16[32,7200]{1,0:T(8,128)(2,1)S(1)} %get-tuple-element.30.refs_0_), channel_id=1, source_target_pairs={{0,32},{16,48},{32,0},{48,16},{64,96},{80,112},{96,64},{112,80},{1... | collective-permute-start | bytes 1382408 | tf_op jit(solution)/shard_map/z0/ppermute | solution.py:37
  14.4 10.0 %slice-start = ((s8[7372800]{0:T(1024)(128)(4,1)}), s8[4194304]{0:T(1024)(128)(4,1)S(1)}, s32[]{:S(2)}) async-start(s8[7372800]{0:T(1024)(128)(4,1)} %bitcast.20), calls=%async_computation.3 | async-start | bytes 8388608
  14.4 10.0 %slice-start.1 = ((s8[7372800]{0:T(1024)(128)(4,1)}), s8[3178496]{0:T(1024)(128)(4,1)S(1)}, s32[]{:S(2)}) async-start(s8[7372800]{0:T(1024)(128)(4,1)} %bitcast.20), calls=%async_computation.4 | async-start | bytes 6356992
  14.4 16.2 %collective-permute-start.5 = (bf16[32,7200]{1,0:T(8,128)(2,1)S(1)}, bf16[32,7200]{1,0:T(8,128)(2,1)S(1)}, u32[]{:S(2)}, u32[]{:S(2)}) collective-permute-start(bf16[32,7200]{1,0:T(8,128)(2,1)S(1)} %collective-permute-done.1.refs_4_), channel_id=1, source_target_pairs={{0,64},{16,80},{32,96},{48,112},{64,128},{80,144},{96,160},{112,17... | collective-permute-start | bytes 1382408 | tf_op jit(solution)/shard_map/l1/ppermute | solution.py:37
  14.5 16.1 %collective-permute-start.4 = (bf16[32,7200]{1,0:T(8,128)(2,1)S(1)}, bf16[32,7200]{1,0:T(8,128)(2,1)S(1)}, u32[]{:S(2)}, u32[]{:S(2)}) collective-permute-start(bf16[32,7200]{1,0:T(8,128)(2,1)S(1)} %collective-permute-done.1.refs_4_), channel_id=1, source_target_pairs={{0,192},{16,208},{32,224},{48,240},{64,0},{80,16},{96,32},{112,48}... | collective-permute-start | bytes 1382408 | tf_op jit(solution)/shard_map/r1/ppermute | solution.py:37
  18.7 25.6 %collective-permute-start.8 = (bf16[32,7200]{1,0:T(8,128)(2,1)S(1)}, bf16[32,7200]{1,0:T(8,128)(2,1)S(1)}, u32[]{:S(2)}, u32[]{:S(2)}) collective-permute-start(bf16[32,7200]{1,0:T(8,128)(2,1)S(1)} %collective-permute-done.1.refs_4_), channel_id=1, source_target_pairs={{0,32},{16,48},{32,0},{48,16},{64,96},{80,112},{96,64},{112,80},{1... | collective-permute-start | bytes 1382408 | tf_op jit(solution)/shard_map/z1/ppermute | solution.py:37
  24.7 39.8 %collective-permute-start.11 = (bf16[900,8,256]{2,1,0:T(8,128)(2,1)S(1)}, bf16[900,8,256]{2,1,0:T(8,128)(2,1)S(1)}, u32[]{:S(2)}, u32[]{:S(2)}) collective-permute-start(bf16[900,8,256]{2,1,0:T(8,128)(2,1)S(1)} %dynamic-slice_bitcast_fusion), channel_id=1, source_target_pairs={{0,16},{16,0},{32,48},{48,32},{64,80},{80,64},{96,112},{112,96},{1... | collective-permute-start | bytes 11059208 | tf_op jit(solution)/shard_map/ints/ppermute | solution.py:37
  30.6 11.0 %collective-permute-start.3 = (bf16[32,7200]{1,0:T(8,128)(2,1)S(1)}, bf16[32,7200]{1,0:T(8,128)(2,1)S(1)}, u32[]{:S(2)}, u32[]{:S(2)}) collective-permute-start(bf16[32,7200]{1,0:T(8,128)(2,1)S(1)} %collective-permute-done.refs_1_), channel_id=1, source_target_pairs={{0,192},{16,208},{32,224},{48,240},{64,0},{80,16},{96,32},{112,48}... | collective-permute-start | bytes 1382408 | tf_op jit(solution)/shard_map/f0/ppermute | solution.py:37
  30.6 13.7 %collective-permute-start.6 = (bf16[32,7200]{1,0:T(8,128)(2,1)S(1)}, bf16[32,7200]{1,0:T(8,128)(2,1)S(1)}, u32[]{:S(2)}, u32[]{:S(2)}) collective-permute-start(bf16[32,7200]{1,0:T(8,128)(2,1)S(1)} %collective-permute-done.5.refs_7_), channel_id=1, source_target_pairs={{0,64},{16,80},{32,96},{48,112},{64,128},{80,144},{96,160},{112,17... | collective-permute-start | bytes 1382408 | tf_op jit(solution)/shard_map/f1/ppermute | solution.py:37
  41.6 11.3 %collective-permute-start.10 = (bf16[32,7200]{1,0:T(8,128)(2,1)S(1)}, bf16[32,7200]{1,0:T(8,128)(2,1)S(1)}, u32[]{:S(2)}, u32[]{:S(2)}) collective-permute-start(bf16[32,7200]{1,0:T(8,128)(2,1)S(1)} %collective-permute-done.7.refs_0_), channel_id=1, source_target_pairs={{0,64},{16,80},{32,96},{48,112},{64,128},{80,144},{96,160},{112,17... | collective-permute-start | bytes 1382408 | tf_op jit(solution)/shard_map/zl0/ppermute | solution.py:37
  41.6 11.3 %collective-permute-start.9 = (bf16[32,7200]{1,0:T(8,128)(2,1)S(1)}, bf16[32,7200]{1,0:T(8,128)(2,1)S(1)}, u32[]{:S(2)}, u32[]{:S(2)}) collective-permute-start(bf16[32,7200]{1,0:T(8,128)(2,1)S(1)} %collective-permute-done.7.refs_0_), channel_id=1, source_target_pairs={{0,192},{16,208},{32,224},{48,240},{64,0},{80,16},{96,32},{112,48}... | collective-permute-start | bytes 1382408 | tf_op jit(solution)/shard_map/zr0/ppermute | solution.py:37
  44.3 16.8 %collective-permute-start.13 = (bf16[32,7200]{1,0:T(8,128)(2,1)S(1)}, bf16[32,7200]{1,0:T(8,128)(2,1)S(1)}, u32[]{:S(2)}, u32[]{:S(2)}) collective-permute-start(bf16[32,7200]{1,0:T(8,128)(2,1)S(1)} %collective-permute-done.8.refs_4_), channel_id=1, source_target_pairs={{0,192},{16,208},{32,224},{48,240},{64,0},{80,16},{96,32},{112,48}... | collective-permute-start | bytes 1382408 | tf_op jit(solution)/shard_map/zr1/ppermute | solution.py:37
  44.6 26.8 %collective-permute-start.15 = (bf16[32,7200]{1,0:T(8,128)(2,1)S(1)}, bf16[32,7200]{1,0:T(8,128)(2,1)S(1)}, u32[]{:S(2)}, u32[]{:S(2)}) collective-permute-start(bf16[32,7200]{1,0:T(8,128)(2,1)S(1)} %collective-permute-done.8.refs_4_), channel_id=1, source_target_pairs={{0,64},{16,80},{32,96},{48,112},{64,128},{80,144},{96,160},{112,17... | collective-permute-start | bytes 1382408 | tf_op jit(solution)/shard_map/zl1/ppermute | solution.py:37
  52.9 0.7 copy-start.1
  52.9 0.7 copy-start.2
  52.9 0.7 copy-start.3
  52.9 18.5 %collective-permute-start.12 = (bf16[32,7200]{1,0:T(8,128)(2,1)S(1)}, bf16[32,7200]{1,0:T(8,128)(2,1)S(1)}, u32[]{:S(2)}, u32[]{:S(2)}) collective-permute-start(bf16[32,7200]{1,0:T(8,128)(2,1)S(1)} %collective-permute-done.10.refs_3_), channel_id=1, source_target_pairs={{0,64},{16,80},{32,96},{48,112},{64,128},{80,144},{96,160},{112,17... | collective-permute-start | bytes 1382408 | tf_op jit(solution)/shard_map/zf0/ppermute | solution.py:37
  61.1 10.3 %collective-permute-start.14 = (bf16[32,7200]{1,0:T(8,128)(2,1)S(1)}, bf16[32,7200]{1,0:T(8,128)(2,1)S(1)}, u32[]{:S(2)}, u32[]{:S(2)}) collective-permute-start(bf16[32,7200]{1,0:T(8,128)(2,1)S(1)} %collective-permute-done.13.refs_5_), channel_id=1, source_target_pairs={{0,192},{16,208},{32,224},{48,240},{64,0},{80,16},{96,32},{112,48}... | collective-permute-start | bytes 1382408 | tf_op jit(solution)/shard_map/zf1/ppermute | solution.py:37
  65.7 5.7 %collective-permute-start.16 = (f32[256,256]{1,0:T(8,128)S(1)}, f32[256,256]{1,0:T(8,128)S(1)}, u32[]{:S(2)}, u32[]{:S(2)}) collective-permute-start(f32[256,256]{1,0:T(8,128)S(1)} %shard_map.71), channel_id=1, source_target_pairs={{0,16},{16,0},{32,48},{48,32},{64,80},{80,64},{96,112},{112,96},{1... | collective-permute-start | bytes 786440 | tf_op jit(solution)/shard_map/t0/ppermute | solution.py:37
  72.6 5.8 %collective-permute-start.17 = (f32[256,256]{1,0:T(8,128)S(1)}, f32[256,256]{1,0:T(8,128)S(1)}, u32[]{:S(2)}, u32[]{:S(2)}) collective-permute-start(f32[256,256]{1,0:T(8,128)S(1)} %shard_map.75), channel_id=1, source_target_pairs={{0,16},{16,0},{32,48},{48,32},{64,80},{80,64},{96,112},{112,96},{1... | collective-permute-start | bytes 786440 | tf_op jit(solution)/shard_map/t1/ppermute | solution.py:37
  78.4 45.4 %copy-start = (bf16[32,256]{1,0:T(8,128)(2,1)S(1)}, bf16[32,256]{1,0:T(8,128)(2,1)}, u32[]{:S(2)}) copy-start(bf16[32,256]{1,0:T(8,128)(2,1)} %other_ref.1) | copy-start | bytes 49156
